TPU v7x, 32 devices: a whole 2x2x4 slice. The times are simulated.
32 devices in a mesh: space: 8 (over z, x), dp: 4 (over y, core).
Axes of the slice: x: 2, y: 2, z: 4, core: 2. Of those that a mesh axis runs over, the one named last changes fastest.
Arguments:
- features: bfloat16 [4, 4096, 128], P('dp', 'space'), may hold values from -6 to 6
- cotangent: bfloat16 [4, 4096, 128], P('dp', 'space'), may hold values from -6 to 6
- weight_one: bfloat16 [27, 128, 128], replicated, may hold values from -0.21875 to 0.21875
- weight_two: bfloat16 [27, 128, 128], replicated, may hold values from -0.21875 to 0.21875
- rules: int32 [4, 8, 2, 27, 256], P('dp', 'space'), may hold values from 0 to 1024, as said below
- halo_send: int32 [4, 8, 2, 2], P('dp', 'space'), may hold values from 0 to 3
- block_counts: int32 [4, 32], P('dp', 'space'), may hold values from 16 to 128
Outputs:
- grad_features: float32 [4, 4096, 128], P('dp', 'space')
- grad_one: float32 [27, 128, 128], replicated
- grad_two: float32 [27, 128, 128], replicated
Inputs may be any that keep to these rules, and one draw needn't show every extreme that they name: `rules`: for each scene, slab and offset, the live slots come first and hold distinct targets and distinct sources; padding slots hold source 1024 and target 512; at least half of the slots are live, and offset 13 is full with each source equal to its target.
All inputs are finite; a program needn't handle non-finite values.
Results may differ from a plain program's by a relative error of at most 0.0032.
Values may be sent and summed in bfloat16 or wider, within the bound.
A program may use at most 64 MiB of HBM per device.

v0:
```python
import jax
import jax.numpy as jnp
from jax import lax
from jax.sharding import PartitionSpec as P


def with_halo(block, sides, width):
    for axis, dim in sides:
        count = lax.axis_size(axis)
        forward = [(i, i + 1) for i in range(count - 1)]
        backward = [(target, source) for source, target in forward]
        low = lax.ppermute(
            lax.slice_in_dim(block, block.shape[dim] - width, None, axis=dim), axis, forward
        )
        high = lax.ppermute(lax.slice_in_dim(block, 0, width, axis=dim), axis, backward)
        block = jnp.concatenate([low, block, high], axis=dim)
    return block


def one_hot_rows(index, count):
    return (index[:, None] == jnp.arange(count, dtype=jnp.int32)[None, :]).astype(jnp.bfloat16)


def lift_rows(selector, table):
    return jnp.dot(selector, table, preferred_element_type=jnp.float32).astype(jnp.bfloat16)


def place_rows(selector, values):
    return jnp.einsum("re,rc->ec", selector, values, preferred_element_type=jnp.float32).astype(
        jnp.bfloat16
    )


def body(features, cotangent, weight_one, weight_two, rules, halo_send, block_counts):
    feats = features[0]
    cot = cotangent[0]
    links = rules[0, 0]
    sends = halo_send[0, 0]
    counts = block_counts[0]
    rows, width = feats.shape
    blocks = counts.shape[0]
    block = rows // blocks
    per_side = sends.shape[1]
    halo_rows = per_side * block
    rule_slots = links.shape[2]
    ext_rows = rows + 2 * halo_rows
    sources = links[0]
    targets = links[1]
    active = (jnp.arange(block)[None, :] < counts[:, None]).astype(jnp.float32).reshape(rows, 1)
    active_half = active.astype(jnp.bfloat16)
    xa = feats * active_half
    ga = cot * active_half
    block_pick = one_hot_rows(sends.reshape(-1), blocks)

    def pick_blocks(table):
        picked = jnp.dot(
            block_pick, table.reshape(blocks, block * width), preferred_element_type=jnp.float32
        )
        return picked.astype(jnp.bfloat16).reshape(2 * halo_rows, width)

    def add_blocks(own, back):
        pieces = jnp.concatenate([back[:halo_rows], back[3 * halo_rows :]], axis=0).reshape(
            2 * per_side, block * width
        )
        added = jnp.einsum(
            "be,bc->ec",
            block_pick.astype(jnp.float32),
            pieces,
            precision=lax.Precision.HIGHEST,
            preferred_element_type=jnp.float32,
        )
        return own + added.reshape(rows, width)

    rim_x = with_halo(pick_blocks(xa), (("space", 0),), halo_rows)
    ext_x = jnp.concatenate([xa, rim_x[:halo_rows], rim_x[3 * halo_rows :]], axis=0)

    def forward_step(total, item):
        src, tgt, weight = item
        placed = place_rows(one_hot_rows(tgt, rows), lift_rows(one_hot_rows(src, ext_rows), ext_x))
        return (total + jnp.dot(placed, weight, preferred_element_type=jnp.float32), None)

    z1, _ = lax.scan(
        forward_step, jnp.zeros((rows, width), jnp.float32), (sources, targets, weight_one)
    )
    y1 = (jax.nn.silu(z1) * active).astype(jnp.bfloat16)
    rim_y = with_halo(pick_blocks(y1), (("space", 0),), halo_rows)
    ext_y = jnp.concatenate([y1, rim_y[:halo_rows], rim_y[3 * halo_rows :]], axis=0)

    def make_backward(table, cot_rows):

        def backward_step(total, item):
            src, tgt, weight = item
            src_pick = one_hot_rows(src, ext_rows)
            cot_picked = lift_rows(one_hot_rows(tgt, rows), cot_rows)
            grad_kernel = jnp.einsum(
                "rc,rd->cd",
                lift_rows(src_pick, table),
                cot_picked,
                preferred_element_type=jnp.float32,
            )
            placed = place_rows(src_pick, cot_picked)
            total = total + jnp.einsum(
                "ed,cd->ec", placed, weight, preferred_element_type=jnp.float32
            )
            return (total, grad_kernel)

        return backward_step

    dext_y, grad_second = lax.scan(
        make_backward(ext_y, ga),
        jnp.zeros((ext_rows, width), jnp.float32),
        (sources, targets, weight_two),
    )
    back_y = with_halo(dext_y[rows:], (("space", 0),), halo_rows)
    dy1 = add_blocks(dext_y[:rows], back_y)
    sig = jax.nn.sigmoid(z1)
    dz1 = (dy1 * sig * (1.0 + z1 * (1.0 - sig)) * active).astype(jnp.bfloat16)
    dext_x, grad_first = lax.scan(
        make_backward(ext_x, dz1),
        jnp.zeros((ext_rows, width), jnp.float32),
        (sources, targets, weight_one),
    )
    back_x = with_halo(dext_x[rows:], (("space", 0),), halo_rows)
    grad_rows = add_blocks(dext_x[:rows], back_x) * active
    total_first, total_second = lax.psum((grad_first, grad_second), ("space", "dp"))
    scale = 1.0 / jnp.sqrt(jnp.float32(lax.axis_size("dp") * lax.axis_size("space") * rule_slots))
    return (grad_rows[None], total_first * scale, total_second * scale)


def solution(mesh):
    in_specs = (
        P("dp", "space", None),
        P("dp", "space", None),
        P(),
        P(),
        P("dp", "space", None, None, None),
        P("dp", "space", None, None),
        P("dp", "space"),
    )
    out_specs = (P("dp", "space", None), P(), P())
    return jax.shard_map(body, mesh=mesh, in_specs=in_specs, out_specs=out_specs, check_vma=False)
```

profile of v0, /device:TPU:0, one launch (start us, length us, event | category | flops | bytes accessed | tf_op | source)
XLA Modules:
  0.0 376.8 jit_solution(5353721253664976763)
XLA Ops:
  11.6 5.5 %collective-permute-start = (bf16[256,128]{1,0:T(8,128)(2,1)S(1)}, bf16[256,128]{1,0:T(8,128)(2,1)S(1)}, u32[]{:S(2)}, u32[]{:S(2)}) collective-permute-start(bf16[256,128]{1,0:T(8,128)(2,1)S(1)} %slice.59), channel_id=1, source_target_pairs={{0,4},{4,8},{8,12},{12,16},{16,20},{20,24},{24,28},{1,5},{5,9},{9,... | collective-permute-start | bytes 196616 | tf_op jit(solution)/shard_map/ppermute | solution.py:12
  19.2 45.4 %while.37 = (s32[]{:T(128)}, f32[512,128]{1,0:T(8,128)S(1)}, s32[27,256]{1,0:T(8,128)S(1)}, s32[27,256]{1,0:T(8,128)S(1)}, bf16[1024,128]{1,0:T(8,128)(2,1)S(1)}...) while((s32[]{:T(128)}, f32[512,128]{1,0:T(8,128)S(1)}, s32[27,256]{1,0:T(8,128)S(1)}, ...), condition=%wide.region_1.2_spmd.clone, body=%wide.region_0.1_spmd.clone.sunk | while | flops 118063104 | bytes 956527 | solution.py:82
  66.6 5.5 %collective-permute-start.2 = (bf16[256,128]{1,0:T(8,128)(2,1)S(1)}, bf16[256,128]{1,0:T(8,128)(2,1)S(1)}, u32[]{:S(2)}, u32[]{:S(2)}) collective-permute-start(bf16[256,128]{1,0:T(8,128)(2,1)S(1)} %slice.63), channel_id=1, source_target_pairs={{0,4},{4,8},{8,12},{12,16},{16,20},{20,24},{24,28},{1,5},{5,9},{9,... | collective-permute-start | bytes 196616 | tf_op jit(solution)/shard_map/ppermute | solution.py:12
  72.4 1.6 collective-permute-done.2
  74.2 64.6 %while.38 = (s32[]{:T(128)}, f32[1024,128]{1,0:T(8,128)S(1)}, f32[27,128,128]{2,1,0:T(8,128)S(1)}, s32[27,256]{1,0:T(8,128)S(1)}, s32[27,256]{1,0:T(8,128)S(1)},...) while((s32[]{:T(128)}, f32[1024,128]{1,0:T(8,128)S(1)}, ...), condition=%wide.region_3.4_spmd.clone, body=%wide.region_2.3_spmd.clone.sunk | while | flops 210829312 | bytes 1744003 | solution.py:109
  76.9 1.5 convolution_add_fusion.7
  79.3 1.5 convolution_add_fusion.7
  81.7 1.5 convolution_add_fusion.7
  84.1 1.5 convolution_add_fusion.7
  86.5 1.5 convolution_add_fusion.7
  88.9 1.5 convolution_add_fusion.7
  91.2 1.5 convolution_add_fusion.7
  93.6 1.5 convolution_add_fusion.7
  96.0 1.5 convolution_add_fusion.7
  100.8 1.5 convolution_add_fusion.7
  103.2 1.5 convolution_add_fusion.7
  105.6 1.5 convolution_add_fusion.7
  108.0 1.5 convolution_add_fusion.7
  110.4 1.5 convolution_add_fusion.7
  112.8 1.5 convolution_add_fusion.7
  115.2 1.5 convolution_add_fusion.7
  117.5 1.5 convolution_add_fusion.7
  119.9 1.5 convolution_add_fusion.7
  122.3 1.5 convolution_add_fusion.7
  124.7 1.5 convolution_add_fusion.7
  127.1 1.5 convolution_add_fusion.7
  129.5 1.5 convolution_add_fusion.7
  131.9 1.5 convolution_add_fusion.7
  134.3 1.5 convolution_add_fusion.7
  136.7 1.5 convolution_add_fusion.7
  138.8 5.0 %collective-permute-start.4 = (f32[256,128]{1,0:T(8,128)S(1)}, f32[256,128]{1,0:T(8,128)S(1)}, u32[]{:S(2)}, u32[]{:S(2)}) collective-permute-start(f32[256,128]{1,0:T(8,128)S(1)} %get-tuple-element.255), channel_id=1, source_target_pairs={{0,4},{4,8},{8,12},{12,16},{16,20},{20,24},{24,28},{1,5},{5,9},{9,... | collective-permute-start | bytes 393224 | tf_op jit(solution)/shard_map/ppermute | solution.py:12
  146.3 5.7 %collective-permute-done.5 = f32[256,128]{1,0:T(8,128)} collective-permute-done((f32[256,128]{1,0:T(8,128)S(1)}, f32[256,128]{1,0:T(8,128)}, u32[]{:S(2)}, u32[]{:S(2)}) %collective-permute-start.5) | collective-permute-done | bytes 131104 | tf_op jit(solution)/shard_map/ppermute | solution.py:15
  152.0 1.6 pad_maximum_fusion.2
  158.1 64.5 %while.39 = (s32[]{:T(128)}, f32[1024,128]{1,0:T(8,128)S(1)}, f32[27,128,128]{2,1,0:T(8,128)S(1)}, s32[27,256]{1,0:T(8,128)S(1)}, s32[27,256]{1,0:T(8,128)S(1)},...) while((s32[]{:T(128)}, f32[1024,128]{1,0:T(8,128)S(1)}, ...), condition=%wide.region_5.6_spmd.clone, body=%wide.region_4.5_spmd.clone.sunk | while | flops 210829312 | bytes 1744003 | solution.py:118
  158.4 1.5 convolution_add_fusion.8
  160.8 1.5 convolution_add_fusion.8
  163.2 1.5 convolution_add_fusion.8
  165.6 1.5 convolution_add_fusion.8
  168.0 1.5 convolution_add_fusion.8
  170.4 1.5 convolution_add_fusion.8
  172.8 1.5 convolution_add_fusion.8
  175.1 1.5 convolution_add_fusion.8
  177.5 1.5 convolution_add_fusion.8
  179.9 1.5 convolution_add_fusion.8
  182.3 1.5 convolution_add_fusion.8
  184.7 1.5 convolution_add_fusion.8
  187.1 1.5 convolution_add_fusion.8
  189.5 1.5 convolution_add_fusion.8
  191.9 1.5 convolution_add_fusion.8
  194.3 1.5 convolution_add_fusion.8
  196.7 1.5 convolution_add_fusion.8
  199.1 1.5 convolution_add_fusion.8
  203.8 1.5 convolution_add_fusion.8
  206.2 1.5 convolution_add_fusion.8
  208.6 1.5 convolution_add_fusion.8
  211.0 1.5 convolution_add_fusion.8
  213.4 1.5 convolution_add_fusion.8
  215.8 1.5 convolution_add_fusion.8
  218.2 1.5 convolution_add_fusion.8
  223.9 4.8 %collective-permute-start.6 = (f32[256,128]{1,0:T(8,128)S(1)}, f32[256,128]{1,0:T(8,128)S(1)}, u32[]{:S(2)}, u32[]{:S(2)}) collective-permute-start(f32[256,128]{1,0:T(8,128)S(1)} %get-tuple-element.253), channel_id=1, source_target_pairs={{0,4},{4,8},{8,12},{12,16},{16,20},{20,24},{24,28},{1,5},{5,9},{9,... | collective-permute-start | bytes 393224 | tf_op jit(solution)/shard_map/ppermute | solution.py:12
  230.1 5.5 %collective-permute-done.6 = f32[256,128]{1,0:T(8,128)S(1)} collective-permute-done((f32[256,128]{1,0:T(8,128)S(1)}, f32[256,128]{1,0:T(8,128)S(1)}, u32[]{:S(2)}, u32[]{:S(2)}) %collective-permute-start.6) | collective-permute-done | bytes 131104 | tf_op jit(solution)/shard_map/ppermute | solution.py:12
  235.6 1.7 collective-permute-done.7
  239.0 126.5 %all-reduce.3.cloned.1.call-done = (f32[27,128,128]{2,1,0:T(8,128)}, f32[27,128,128]{2,1,0:T(8,128)}) async-done(((f32[27,128,128]{2,1,0:T(8,128)}, f32[27,128,128]{2,1,0:T(8,128)}), (f32[27,128,128]{2,1,0:T(8,128)}, f32[27,128,128]{2,1,0:T(8,128)})) %all-reduce.3.cloned.1.call-update) | async-done | bytes 3538960 | tf_op jit(solution)/shard_map/psum | solution.py:125
  365.5 3.1 broadcast_multiply_fusion.1
  (303 shorter events, 117.8 us)
Async XLA Ops:
  7.2 358.3 %all-reduce.3.cloned.1.call-start = ((), (), s32[]{:S(2)}) async-start(), calls=%async_computation | async-start | bytes 7077888 | tf_op jit(solution)/shard_map/psum | solution.py:125
  10.2 8.9 %collective-permute-start.1 = (bf16[256,128]{1,0:T(8,128)(2,1)S(1)}, bf16[256,128]{1,0:T(8,128)(2,1)S(1)}, u32[]{:S(2)}, u32[]{:S(2)}) collective-permute-start(bf16[256,128]{1,0:T(8,128)(2,1)S(1)} %slice.61), channel_id=1, source_target_pairs={{4,0},{8,4},{12,8},{16,12},{20,16},{24,20},{28,24},{5,1},{9,5},{13... | collective-permute-start | bytes 196616 | tf_op jit(solution)/shard_map/ppermute | solution.py:15
  11.6 7.6 %collective-permute-start = (bf16[256,128]{1,0:T(8,128)(2,1)S(1)}, bf16[256,128]{1,0:T(8,128)(2,1)S(1)}, u32[]{:S(2)}, u32[]{:S(2)}) collective-permute-start(bf16[256,128]{1,0:T(8,128)(2,1)S(1)} %slice.59), channel_id=1, source_target_pairs={{0,4},{4,8},{8,12},{12,16},{16,20},{20,24},{24,28},{1,5},{5,9},{9,... | collective-permute-start | bytes 196616 | tf_op jit(solution)/shard_map/ppermute | solution.py:12
  64.6 9.6 %copy-start.3 = (bf16[1024,128]{1,0:T(8,128)(2,1)}, bf16[1024,128]{1,0:T(8,128)(2,1)S(1)}, u32[]{:S(2)}) copy-start(bf16[1024,128]{1,0:T(8,128)(2,1)S(1)} %get-tuple-element.511) | copy-start | bytes 786436
  65.3 7.1 %collective-permute-start.3 = (bf16[256,128]{1,0:T(8,128)(2,1)S(1)}, bf16[256,128]{1,0:T(8,128)(2,1)S(1)}, u32[]{:S(2)}, u32[]{:S(2)}) collective-permute-start(bf16[256,128]{1,0:T(8,128)(2,1)S(1)} %slice.65), channel_id=1, source_target_pairs={{4,0},{8,4},{12,8},{16,12},{20,16},{24,20},{28,24},{5,1},{9,5},{13... | collective-permute-start | bytes 196616 | tf_op jit(solution)/shard_map/ppermute | solution.py:15
  66.6 7.4 %collective-permute-start.2 = (bf16[256,128]{1,0:T(8,128)(2,1)S(1)}, bf16[256,128]{1,0:T(8,128)(2,1)S(1)}, u32[]{:S(2)}, u32[]{:S(2)}) collective-permute-start(bf16[256,128]{1,0:T(8,128)(2,1)S(1)} %slice.63), channel_id=1, source_target_pairs={{0,4},{4,8},{8,12},{12,16},{16,20},{20,24},{24,28},{1,5},{5,9},{9,... | collective-permute-start | bytes 196616 | tf_op jit(solution)/shard_map/ppermute | solution.py:12
  138.8 18.2 %copy-start.1 = (f32[27,128,128]{2,1,0:T(8,128)}, f32[27,128,128]{2,1,0:T(8,128)S(1)}, u32[]{:S(2)}) copy-start(f32[27,128,128]{2,1,0:T(8,128)S(1)} %get-tuple-element.125) | copy-start | bytes 5308420
  138.8 7.5 %collective-permute-start.4 = (f32[256,128]{1,0:T(8,128)S(1)}, f32[256,128]{1,0:T(8,128)S(1)}, u32[]{:S(2)}, u32[]{:S(2)}) collective-permute-start(f32[256,128]{1,0:T(8,128)S(1)} %get-tuple-element.255), channel_id=1, source_target_pairs={{0,4},{4,8},{8,12},{12,16},{16,20},{20,24},{24,28},{1,5},{5,9},{9,... | collective-permute-start | bytes 393224 | tf_op jit(solution)/shard_map/ppermute | solution.py:12
  143.8 8.2 %collective-permute-start.5 = (f32[256,128]{1,0:T(8,128)S(1)}, f32[256,128]{1,0:T(8,128)}, u32[]{:S(2)}, u32[]{:S(2)}) collective-permute-start(f32[256,128]{1,0:T(8,128)S(1)} %get-tuple-element.256), channel_id=1, source_target_pairs={{4,0},{8,4},{12,8},{16,12},{20,16},{24,20},{28,24},{5,1},{9,5},{13... | collective-permute-start | bytes 393224 | tf_op jit(solution)/shard_map/ppermute | solution.py:15
  157.2 1.0 copy-start.4
  222.7 1.2 copy-start
  223.9 11.7 %collective-permute-start.6 = (f32[256,128]{1,0:T(8,128)S(1)}, f32[256,128]{1,0:T(8,128)S(1)}, u32[]{:S(2)}, u32[]{:S(2)}) collective-permute-start(f32[256,128]{1,0:T(8,128)S(1)} %get-tuple-element.253), channel_id=1, source_target_pairs={{0,4},{4,8},{8,12},{12,16},{16,20},{20,24},{24,28},{1,5},{5,9},{9,... | collective-permute-start | bytes 393224 | tf_op jit(solution)/shard_map/ppermute | solution.py:12
  228.8 8.5 %collective-permute-start.7 = (f32[256,128]{1,0:T(8,128)S(1)}, f32[256,128]{1,0:T(8,128)S(1)}, u32[]{:S(2)}, u32[]{:S(2)}) collective-permute-start(f32[256,128]{1,0:T(8,128)S(1)} %get-tuple-element.254), channel_id=1, source_target_pairs={{4,0},{8,4},{12,8},{16,12},{20,16},{24,20},{28,24},{5,1},{9,5},{13... | collective-permute-start | bytes 393224 | tf_op jit(solution)/shard_map/ppermute | solution.py:15
  365.5 3.1 copy-start.2
Sparse Core Ops, SparseCore 0:
  224.0 141.3 all-reduce.2
where the time goes:
time: 383 us; the launch traced here: 377 us
  matrix products  173 us (45%)
  waiting for transfers between devices  143 us (37%)
  starting transfers between devices  25.9 us (7%)
  between operations  14.4 us (4%)
  other arithmetic  9.1 us (2%)
  local copies, waits for them, and re-layouts  9.04 us (2%)
    psum x1, waiting for transfers between devices, body(): lax.psum((grad_first, grad_second), ('space', 'dp'))  126 us
    dot_general x54, matrix products, backward_step(): jnp.einsum('ed,cd->ec', placed, weight, preferred_element_type=jnp.float32)  81.1 us
    dot_general x27, matrix products, forward_step(): jnp.dot(placed, weight, preferred_element_type=jnp.float32)  34.5 us
    dot_general x54, matrix products, backward_step(): jnp.einsum('rc,rd->cd', lift_rows(src_pick, table), cot_picked, preferred...  30.3 us
    dot_general x81, matrix products, lift_rows(): jnp.dot(selector, table, preferred_element_type=jnp.float32)  24.5 us
    ppermute x4, starting transfers between devices, with_halo(): lax.ppermute(lax.slice_in_dim(block, block.shape[dim] - width, None, axis...  20.7 us
    ppermute x4, waiting for transfers between devices, with_halo(): lax.ppermute(lax.slice_in_dim(block, block.shape[dim] - width, None, axis...  8.31 us
    ppermute x4, waiting for transfers between devices, with_halo(): lax.ppermute(lax.slice_in_dim(block, 0, width, axis=dim), axis, backward)  7.7 us
  transfers between devices with their start and end apart: 9, of which 7 were waited for; matrix products, arithmetic and copies ran while one was open for 1% of the time, Pallas kernels for 0%

commit v1 on v0

v1 whole, which is shorter than its diff:
```python
import functools

import jax
import jax.numpy as jnp
from jax import lax
from jax.experimental import pallas as pl
from jax.experimental.pallas import tpu as pltpu
from jax.sharding import PartitionSpec as P

F32 = jnp.float32
BF16 = jnp.bfloat16
CHUNK = 256
GROUP = 3
VMEM_LIMIT = 48 * 1024 * 1024


def dot(a, b):
    return jnp.dot(a, b, preferred_element_type=F32)


def dot_nt(a, b):
    return lax.dot_general(a, b, (((1,), (1,)), ((), ())), preferred_element_type=F32)


def dot_tn(a, b):
    return lax.dot_general(a, b, (((0,), (0,)), ((), ())), preferred_element_type=F32)


def one_hot(index_row, count):
    slots = index_row.shape[1]
    index = index_row.astype(F32)
    rows = lax.broadcasted_iota(jnp.int32, (CHUNK, slots), 0).astype(F32).astype(BF16)
    one, zero = jnp.ones((), BF16), jnp.zeros((), BF16)
    parts = []
    for base in range(0, count, CHUNK):
        shifted = jnp.broadcast_to((index - base).astype(BF16), (CHUNK, slots))
        parts.append(jnp.where(rows == shifted, one, zero))
    return jnp.concatenate(parts, axis=0)


def active_mask(counts_ref, blocks, block, width):
    lane = lax.broadcasted_iota(jnp.int32, (width, block), 1)
    return [(lane < counts_ref[0, b]).astype(F32) for b in range(blocks)]


def pick(sends_ref, side, per_side, table, blocks, block):
    picked = []
    for j in range(per_side):
        total = 0.0
        for b in range(blocks):
            total = total + jnp.where(
                sends_ref[side, j] == b, table[:, b * block : (b + 1) * block], 0.0
            )
        picked.append(total)
    return jnp.concatenate(picked, axis=1)


def add_back(own, sends_ref, per_side, from_left, from_right, blocks, block):
    out = []
    for b in range(blocks):
        total = own[:, b * block : (b + 1) * block]
        for side, back in ((0, from_left), (1, from_right)):
            for j in range(per_side):
                total = total + jnp.where(
                    sends_ref[side, j] == b, back[:, j * block : (j + 1) * block], 0.0
                )
        out.append(total)
    return jnp.concatenate(out, axis=1)


def prep_kernel(dims, feats, cot, counts, sends, xa_t, ga_t, low, high):
    blocks, block, per_side = dims
    width = feats.shape[1]
    mask = jnp.concatenate(active_mask(counts, blocks, block, width), axis=1)
    xa = feats[...].astype(F32).T * mask
    xa_t[...] = xa.astype(BF16)
    ga_t[...] = (cot[...].astype(F32).T * mask).astype(BF16)
    low[...] = pick(sends, 0, per_side, xa, blocks, block).astype(BF16)
    high[...] = pick(sends, 1, per_side, xa, blocks, block).astype(BF16)


def back_two_kernel(ga_t, rules, weight, dext, gga):
    width, rows = ga_t.shape
    ext_rows = dext.shape[1]
    kernels = weight.shape[0]
    dext[...] = jnp.zeros_like(dext)

    def step(i, _):
        weights, placed = [], []
        for j in range(GROUP):
            k = i * GROUP + j
            gathered = dot(ga_t[...], one_hot(rules[1, pl.ds(k, 1), :], rows)).astype(BF16)
            gga[k] = gathered
            placed.append(
                dot_nt(gathered, one_hot(rules[0, pl.ds(k, 1), :], ext_rows)).astype(BF16)
            )
            weights.append(weight[k])
        dext[...] += dot(jnp.concatenate(weights, axis=1), jnp.concatenate(placed, axis=0))
        return 0

    lax.fori_loop(0, kernels // GROUP, step, 0)


def forward_kernel(dims, xa_t, left, right, rules, weight, counts, sends, gx, y_t, slope, low, high, ext, z):
    blocks, block, per_side = dims
    width, rows = xa_t.shape
    halo = left.shape[1]
    ext_rows = ext.shape[1]
    kernels = weight.shape[0]
    ext[:, :rows] = xa_t[...]
    ext[:, rows : rows + halo] = left[...]
    ext[:, rows + halo :] = right[...]
    z[...] = jnp.zeros_like(z)

    def step(i, _):
        weights, placed = [], []
        for j in range(GROUP):
            k = i * GROUP + j
            gathered = dot(ext[...], one_hot(rules[0, pl.ds(k, 1), :], ext_rows)).astype(BF16)
            gx[k] = gathered
            placed.append(dot_nt(gathered, one_hot(rules[1, pl.ds(k, 1), :], rows)).astype(BF16))
            weights.append(weight[k])
        z[...] += dot_tn(jnp.concatenate(weights, axis=0), jnp.concatenate(placed, axis=0))
        return 0

    lax.fori_loop(0, kernels // GROUP, step, 0)
    mask = jnp.concatenate(active_mask(counts, blocks, block, width), axis=1)
    zv = z[...]
    sig = 1.0 / (1.0 + jnp.exp(-zv))
    y = ((zv * sig) * mask).astype(BF16)
    y_t[...] = y
    y32 = y.astype(F32)
    slope[...] = sig * (1.0 + zv * (1.0 - sig)) * mask
    low[...] = pick(sends, 0, per_side, y32, blocks, block).astype(BF16)
    high[...] = pick(sends, 1, per_side, y32, blocks, block).astype(BF16)


def back_one_kernel(dims, dext_y, back_left, back_right, slope, sends, rules, weight, gx, dext, grad, dz):
    blocks, block, per_side = dims
    width, rows = slope.shape
    ext_rows = dext.shape[1]
    kernels = weight.shape[0]
    dy = add_back(
        dext_y[:, :rows], sends, per_side, back_left[...], back_right[...], blocks, block
    )
    dz[...] = (dy * slope[...]).astype(BF16)
    dext[...] = jnp.zeros_like(dext)

    def step(i, _):
        products, selectors = [], []
        for j in range(GROUP):
            k = i * GROUP + j
            gathered = dot(dz[...], one_hot(rules[1, pl.ds(k, 1), :], rows)).astype(BF16)
            grad[k] = dot_nt(gx[k], gathered)
            products.append(dot(weight[k], gathered).astype(BF16))
            selectors.append(one_hot(rules[0, pl.ds(k, 1), :], ext_rows))
        dext[...] += dot_nt(jnp.concatenate(products, axis=1), jnp.concatenate(selectors, axis=1))
        return 0

    lax.fori_loop(0, kernels // GROUP, step, 0)


def grad_two_kernel(y_t, left, right, rules, gga, grad, ext):
    width, rows = y_t.shape
    halo = left.shape[1]
    ext_rows = ext.shape[1]
    kernels = gga.shape[0]
    ext[:, :rows] = y_t[...]
    ext[:, rows : rows + halo] = left[...]
    ext[:, rows + halo :] = right[...]

    def step(i, _):
        for j in range(GROUP):
            k = i * GROUP + j
            gathered = dot(ext[...], one_hot(rules[0, pl.ds(k, 1), :], ext_rows)).astype(BF16)
            grad[k] = dot_nt(gathered, gga[k])
        return 0

    lax.fori_loop(0, kernels // GROUP, step, 0)


def finish_kernel(dims, dext, back_left, back_right, counts, sends, out):
    blocks, block, per_side = dims
    rows, width = out.shape
    own = add_back(
        dext[:, :rows], sends, per_side, back_left[...], back_right[...], blocks, block
    )
    mask = jnp.concatenate(active_mask(counts, blocks, block, width), axis=1)
    out[...] = (own * mask).T


def call(kernel, kinds, outs, scratch=()):
    spaces = {"v": pltpu.VMEM, "s": pltpu.SMEM}
    return pl.pallas_call(
        kernel,
        out_shape=[jax.ShapeDtypeStruct(shape, dtype) for shape, dtype in outs],
        in_specs=[pl.BlockSpec(memory_space=spaces[kind]) for kind in kinds],
        out_specs=[pl.BlockSpec(memory_space=pltpu.VMEM) for _ in outs],
        scratch_shapes=list(scratch),
        compiler_params=pltpu.CompilerParams(vmem_limit_bytes=VMEM_LIMIT),
    )


def body(features, cotangent, weight_one, weight_two, rules, halo_send, block_counts):
    feats, cot, links, sends, counts = (
        features[0], cotangent[0], rules[0, 0], halo_send[0, 0], block_counts
    )
    rows, width = feats.shape
    blocks = counts.shape[1]
    block = rows // blocks
    per_side = sends.shape[1]
    halo = per_side * block
    kernels, slots = links.shape[1:]
    ext_rows = rows + 2 * halo
    dims = (blocks, block, per_side)
    count = lax.axis_size("space")
    up = [(i, i + 1) for i in range(count - 1)]
    down = [(t, s) for s, t in up]

    def swap(to_low, to_high):
        return lax.ppermute(to_high, "space", up), lax.ppermute(to_low, "space", down)

    xa_t, ga_t, x_low, x_high = call(
        functools.partial(prep_kernel, dims),
        "vvss",
        [((width, rows), BF16)] * 2 + [((width, halo), BF16)] * 2,
    )(feats, cot, counts, sends)
    x_left, x_right = swap(x_low, x_high)
    dext_y, gga = call(
        back_two_kernel,
        "vvv",
        [((width, ext_rows), F32), ((kernels, width, slots), BF16)],
    )(ga_t, links, weight_two)
    dy_left, dy_right = swap(dext_y[:, rows : rows + halo], dext_y[:, rows + halo :])
    gx, y_t, slope, y_low, y_high = call(
        functools.partial(forward_kernel, dims),
        "vvvvvss",
        [((kernels, width, slots), BF16), ((width, rows), BF16), ((width, rows), F32)]
        + [((width, halo), BF16)] * 2,
        [pltpu.VMEM((width, ext_rows), BF16), pltpu.VMEM((width, rows), F32)],
    )(xa_t, x_left, x_right, links, weight_one, counts, sends)
    y_left, y_right = swap(y_low, y_high)
    dext_x, grad_one = call(
        functools.partial(back_one_kernel, dims),
        "vvvvsvvv",
        [((width, ext_rows), F32), ((kernels, width, width), F32)],
        [pltpu.VMEM((width, rows), BF16)],
    )(dext_y, dy_left, dy_right, slope, sends, links, weight_one, gx)
    dx_left, dx_right = swap(dext_x[:, rows : rows + halo], dext_x[:, rows + halo :])
    total_one = lax.psum(grad_one, ("space", "dp"))
    (grad_two,) = call(
        grad_two_kernel,
        "vvvvv",
        [((kernels, width, width), F32)],
        [pltpu.VMEM((width, ext_rows), BF16)],
    )(y_t, y_left, y_right, links, gga)
    total_two = lax.psum(grad_two, ("space", "dp"))
    (grad_rows,) = call(
        functools.partial(finish_kernel, dims), "vvvss", [((rows, width), F32)]
    )(dext_x, dx_left, dx_right, counts, sends)
    scale = 1.0 / jnp.sqrt(F32(lax.axis_size("dp") * count * slots))
    return (grad_rows[None], total_one * scale, total_two * scale)


def solution(mesh):
    in_specs = (
        P("dp", "space", None),
        P("dp", "space", None),
        P(),
        P(),
        P("dp", "space", None, None, None),
        P("dp", "space", None, None),
        P("dp", "space"),
    )
    out_specs = (P("dp", "space", None), P(), P())
    return jax.shard_map(body, mesh=mesh, in_specs=in_specs, out_specs=out_specs, check_vma=False)
```

time: 383 us -> 228 us (0.60); the launches traced: 377 us -> 228 us
  matrix products: 173 us -> 0 us
  Pallas kernels: 0 us -> 41.3 us
  other arithmetic: 9.1 us -> 4.39 us
  waiting for transfers between devices: 143 us -> 139 us
    dot_general x220 -> x0, matrix products: 173 us -> none  [the longest x54 81.1 us: backward_step(): jnp.einsum('ed,cd->ec', placed, weight, preferred_element_type=jnp.float32)]
    pallas_call x0 -> x6, Pallas kernels: none -> 41.3 us  [the longest x1 10.5 us: body(): call(back_two_kernel, 'vvv', [((width, ext_rows), F32), ((kernels, width,...]
    ppermute x8, waiting for transfers between devices: 16 us -> 11.2 us  [the longest x4 7.14 us: swap(): lax.ppermute(to_low, 'space', down)]
    unnamed x11 -> x21, local copies, waits for them, and re-layouts: 2.1 us -> 6.54 us
  transfers between devices with their start and end apart: 9 -> 9, of which waited for: 7 -> 4; matrix products, arithmetic and copies ran while one was open for 1% -> 0% of each run, Pallas kernels for 0% -> 9%
where the time goes in v1:
time: 228 us
  waiting for transfers between devices  139 us (61%)
  Pallas kernels  41.3 us (18%)
  starting transfers between devices  22.2 us (10%)
  between operations  14.2 us (6%)
  local copies, waits for them, and re-layouts  6.58 us (3%)
  other arithmetic  4.39 us (2%)
    psum x1, waiting for transfers between devices, body(): total_one = lax.psum(grad_one, ('space', 'dp'))  128 us
    ppermute x4, starting transfers between devices, swap(): lax.ppermute(to_high, 'space', up)  17 us
    pallas_call x1, Pallas kernels, body(): call(back_two_kernel, 'vvv', [((width, ext_rows), F32), ((kernels, width,...  10.5 us
    pallas_call x1, Pallas kernels, body(): call(functools.partial(back_one_kernel, dims), 'vvvvsvvv', [((width, ext_...  10.2 us
    pallas_call x1, Pallas kernels, body(): call(grad_two_kernel, 'vvvvv', [((kernels, width, width), F32)], [pltpu.V...  9.37 us
    pallas_call x1, Pallas kernels, body(): call(functools.partial(forward_kernel, dims), 'vvvvvss', [((kernels, widt...  9.09 us
    ppermute x4, waiting for transfers between devices, swap(): lax.ppermute(to_low, 'space', down)  7.14 us
    unnamed x21, local copies, waits for them, and re-layouts  6.54 us
  transfers between devices with their start and end apart: 9, of which 4 were waited for; matrix products, arithmetic and copies ran while one was open for 0% of the time, Pallas kernels for 9%

profile of v1, /device:TPU:0, one launch (start us, length us, event | category | flops | bytes accessed | tf_op | source)
XLA Modules:
  0.0 227.8 jit_solution(10116221936312714548)
XLA Ops:
  7.2 0.0 copy-start
  7.2 0.0 all-reduce.3.cloned.1.call-start
  7.2 0.9 copy.12
  8.1 0.0 copy-start.2
  8.1 0.9 copy-done.2
  9.0 0.0 copy-start.3
  9.0 0.9 copy-done.3
  9.9 0.0 copy-start.4
  9.9 0.7 copy-done.4
  10.6 0.0 copy-start.7
  10.6 0.7 copy-done.7
  11.3 0.7 shard_map.94
  12.0 0.0 copy-start.1
  12.0 1.2 copy-done.1
  13.2 10.5 %shard_map.95 = (f32[128,1024]{1,0:T(8,128)S(1)}, bf16[27,128,256]{2,1,0:T(8,128)(2,1)S(1)}) custom-call(bf16[128,512]{1,0:T(8,128)(2,1)S(1)} %get-tuple-element.16.ga_t, s32[2,27,256]{2,1,0:T(8,128)S(1)} %bitcast.7, bf16[27,128,128]{2,1,0:T(8,128)(2,1)S(1)} %copy-done.1), custom_call_target="tpu_custom_call" | custom-call | tf_op jit(solution)/shard_map/pallas_call | solution.py:229
  23.7 4.8 %collective-permute-start = (f32[128,256]{1,0:T(8,128)S(1)}, f32[128,256]{1,0:T(8,128)S(1)}, u32[]{:S(2)}, u32[]{:S(2)}) collective-permute-start(f32[128,256]{1,0:T(8,128)S(1)} %get-tuple-element.34), channel_id=1, source_target_pairs={{0,4},{4,8},{8,12},{12,16},{16,20},{20,24},{24,28},{1,5},{5,9},{9,... | collective-permute-start | bytes 393224 | tf_op jit(solution)/shard_map/ppermute | solution.py:221
  28.5 3.5 %collective-permute-start.2 = (bf16[128,256]{1,0:T(8,128)(2,1)S(1)}, bf16[128,256]{1,0:T(8,128)(2,1)S(1)}, u32[]{:S(2)}, u32[]{:S(2)}) collective-permute-start(bf16[128,256]{1,0:T(8,128)(2,1)S(1)} %get-tuple-element.19), channel_id=1, source_target_pairs={{0,4},{4,8},{8,12},{12,16},{16,20},{20,24},{24,28},{1,5},{5,9},{9,... | collective-permute-start | bytes 196616 | tf_op jit(solution)/shard_map/ppermute | solution.py:221
  32.0 1.3 collective-permute-start.3
  33.3 1.3 collective-permute-start.1
  34.6 0.0 collective-permute-done.2.left
  34.6 4.0 %collective-permute-done.3.right = bf16[128,256]{1,0:T(8,128)(2,1)S(1)} collective-permute-done((bf16[128,256]{1,0:T(8,128)(2,1)S(1)}, bf16[128,256]{1,0:T(8,128)(2,1)S(1)}, u32[]{:S(2)}, u32[]{:S(2)}) %collective-permute-start.3) | collective-permute-done | bytes 65568 | tf_op jit(solution)/shard_map/ppermute | solution.py:221
  38.6 0.0 copy-done
  38.6 0.0 copy-start.5
  38.6 0.7 copy-done.5
  39.3 0.0 copy-start.8
  39.3 0.7 copy-done.8
  40.0 9.1 %shard_map.96 = (bf16[27,128,256]{2,1,0:T(8,128)(2,1)S(1)}, bf16[128,512]{1,0:T(8,128)(2,1)S(1)}, f32[128,512]{1,0:T(8,128)S(1)}, bf16[128,256]{1,0:T(8,128)(2,1)S(1)}, bf16[128,256]{1,0:T(8,128)(2,1)S(1)}) custom-call(bf16[128,512]{1,0:T(8,128)(2,1)S(1)} %get-tuple-element.18.xa_t, bf16[128,256]{1,0:T(8,128)(2,1)S(1)} %collective-permute-done.2.left, ...), custom_call_target="tpu_custom_call" | custom-call | tf_op jit(solution)/shard_map/pallas_call | solution.py:235
  49.1 4.1 %collective-permute-start.6 = (bf16[128,256]{1,0:T(8,128)(2,1)S(1)}, bf16[128,256]{1,0:T(8,128)(2,1)S(1)}, u32[]{:S(2)}, u32[]{:S(2)}) collective-permute-start(bf16[128,256]{1,0:T(8,128)(2,1)S(1)} %get-tuple-element.26), channel_id=1, source_target_pairs={{0,4},{4,8},{8,12},{12,16},{16,20},{20,24},{24,28},{1,5},{5,9},{9,... | collective-permute-start | bytes 196616 | tf_op jit(solution)/shard_map/ppermute | solution.py:221
  53.2 1.3 collective-permute-start.7
  54.5 0.0 collective-permute-done.back_left
  54.5 0.0 collective-permute-done.1.back_right
  54.5 10.2 %shard_map.97 = (f32[128,1024]{1,0:T(8,128)S(1)}, f32[27,128,128]{2,1,0:T(8,128)}) custom-call(f32[128,1024]{1,0:T(8,128)S(1)} %get-tuple-element.17.dext_y, f32[128,256]{1,0:T(8,128)S(1)} %collective-permute-done.back_left, f32[128,256]{1,0:T(8,128)S(1)} %collective-permute-done.1.back_right, f32[128,512]{1,0:T(8,128)S(1)} %get-tuple-element.21.slope, ...), custom_call_target="tpu_custom_call" | custom-call | tf_op jit(solution)/shard_map/pallas_call | solution.py:243
  64.8 0.0 collective-permute-done.6.left
  64.8 0.0 collective-permute-done.7.right
  64.8 9.4 %shard_map.99 = f32[27,128,128]{2,1,0:T(8,128)} custom-call(bf16[128,512]{1,0:T(8,128)(2,1)S(1)} %get-tuple-element.25.y_t, bf16[128,256]{1,0:T(8,128)(2,1)S(1)} %collective-permute-done.6.left, bf16[128,256]{1,0:T(8,128)(2,1)S(1)} %collective-permute-done.7.right, s32[2,27,256]{2,1,0:T(8,128)S(1)} %bitcast.10, bf16[27,128,256]{2,1,0:T(8,128)(2,1)S(1)} %get-tuple-element.28.gga), custom_call_target="tpu_custom_call" | custom-call | tf_op jit(solution)/shard_map/pallas_call | solution.py:251
  74.1 0.0 copy-start.6
  74.1 0.0 copy-start.9
  74.1 0.0 all-reduce.3.cloned.1.call-update
  74.2 4.6 %collective-permute-start.4 = (f32[128,256]{1,0:T(8,128)S(1)}, f32[128,256]{1,0:T(8,128)S(1)}, u32[]{:S(2)}, u32[]{:S(2)}) collective-permute-start(f32[128,256]{1,0:T(8,128)S(1)} %get-tuple-element.32), channel_id=1, source_target_pairs={{0,4},{4,8},{8,12},{12,16},{16,20},{20,24},{24,28},{1,5},{5,9},{9,... | collective-permute-start | bytes 393224 | tf_op jit(solution)/shard_map/ppermute | solution.py:221
  78.8 1.3 collective-permute-start.5
  80.0 4.0 %collective-permute-done.4.back_left = f32[128,256]{1,0:T(8,128)S(1)} collective-permute-done((f32[128,256]{1,0:T(8,128)S(1)}, f32[128,256]{1,0:T(8,128)S(1)}, u32[]{:S(2)}, u32[]{:S(2)}) %collective-permute-start.4) | collective-permute-done | bytes 131104 | tf_op jit(solution)/shard_map/ppermute | solution.py:221
  84.1 3.1 %collective-permute-done.5.back_right = f32[128,256]{1,0:T(8,128)S(1)} collective-permute-done((f32[128,256]{1,0:T(8,128)S(1)}, f32[128,256]{1,0:T(8,128)S(1)}, u32[]{:S(2)}, u32[]{:S(2)}) %collective-permute-start.5) | collective-permute-done | bytes 131104 | tf_op jit(solution)/shard_map/ppermute | solution.py:221
  87.2 0.0 copy-done.6
  87.2 0.0 copy-done.9
  87.2 1.4 shard_map.98
  88.6 128.0 %all-reduce.3.cloned.1.call-done = (f32[27,128,128]{2,1,0:T(8,128)}, f32[27,128,128]{2,1,0:T(8,128)}) async-done(((f32[27,128,128]{2,1,0:T(8,128)}, f32[27,128,128]{2,1,0:T(8,128)}), (f32[27,128,128]{2,1,0:T(8,128)}, f32[27,128,128]{2,1,0:T(8,128)})) %all-reduce.3.cloned.1.call-update) | async-done | bytes 3538960 | tf_op jit(solution)/shard_map/psum | solution.py:250
  216.6 4.4 %broadcast_multiply_fusion = (f32[27,128,128]{2,1,0:T(8,128)}, f32[27,128,128]{2,1,0:T(8,128)}) fusion(f32[27,128,128]{2,1,0:T(8,128)} %get-tuple-element.30, f32[27,128,128]{2,1,0:T(8,128)} %get-tuple-element.29), kind=kLoop, calls=%fused_computation | loop fusion | flops 884736 | bytes 7077888 | tf_op jit(solution)/shard_map/mul | solution.py:262
  (2 shorter events, 0.0 us)
Async XLA Ops:
  7.2 31.5 %copy-start = (bf16[27,128,128]{2,1,0:T(8,128)(2,1)S(1)}, bf16[27,128,128]{2,1,0:T(8,128)(2,1)}, u32[]{:S(2)}) copy-start(bf16[27,128,128]{2,1,0:T(8,128)(2,1)} %weight.5) | copy-start | bytes 2654212
  7.2 209.4 %all-reduce.3.cloned.1.call-start = ((), (), s32[]{:S(2)}) async-start(), calls=%async_computation | async-start | bytes 7077888 | tf_op jit(solution)/shard_map/psum | solution.py:250
  8.1 0.9 copy-start.2
  9.0 0.9 copy-start.3
  9.9 0.7 copy-start.4
  10.6 0.7 copy-start.7
  12.0 1.2 copy-start.1
  23.7 30.8 %collective-permute-start = (f32[128,256]{1,0:T(8,128)S(1)}, f32[128,256]{1,0:T(8,128)S(1)}, u32[]{:S(2)}, u32[]{:S(2)}) collective-permute-start(f32[128,256]{1,0:T(8,128)S(1)} %get-tuple-element.34), channel_id=1, source_target_pairs={{0,4},{4,8},{8,12},{12,16},{16,20},{20,24},{24,28},{1,5},{5,9},{9,... | collective-permute-start | bytes 393224 | tf_op jit(solution)/shard_map/ppermute | solution.py:221
  28.5 6.1 %collective-permute-start.2 = (bf16[128,256]{1,0:T(8,128)(2,1)S(1)}, bf16[128,256]{1,0:T(8,128)(2,1)S(1)}, u32[]{:S(2)}, u32[]{:S(2)}) collective-permute-start(bf16[128,256]{1,0:T(8,128)(2,1)S(1)} %get-tuple-element.19), channel_id=1, source_target_pairs={{0,4},{4,8},{8,12},{12,16},{16,20},{20,24},{24,28},{1,5},{5,9},{9,... | collective-permute-start | bytes 196616 | tf_op jit(solution)/shard_map/ppermute | solution.py:221
  32.0 6.6 %collective-permute-start.3 = (bf16[128,256]{1,0:T(8,128)(2,1)S(1)}, bf16[128,256]{1,0:T(8,128)(2,1)S(1)}, u32[]{:S(2)}, u32[]{:S(2)}) collective-permute-start(bf16[128,256]{1,0:T(8,128)(2,1)S(1)} %get-tuple-element.20), channel_id=1, source_target_pairs={{4,0},{8,4},{12,8},{16,12},{20,16},{24,20},{28,24},{5,1},{9,5},{13... | collective-permute-start | bytes 196616 | tf_op jit(solution)/shard_map/ppermute | solution.py:221
  33.3 21.2 %collective-permute-start.1 = (f32[128,256]{1,0:T(8,128)S(1)}, f32[128,256]{1,0:T(8,128)S(1)}, u32[]{:S(2)}, u32[]{:S(2)}) collective-permute-start(f32[128,256]{1,0:T(8,128)S(1)} %get-tuple-element.33), channel_id=1, source_target_pairs={{4,0},{8,4},{12,8},{16,12},{20,16},{24,20},{28,24},{5,1},{9,5},{13... | collective-permute-start | bytes 393224 | tf_op jit(solution)/shard_map/ppermute | solution.py:221
  38.6 0.7 copy-start.5
  39.3 0.7 copy-start.8
  49.1 15.7 %collective-permute-start.6 = (bf16[128,256]{1,0:T(8,128)(2,1)S(1)}, bf16[128,256]{1,0:T(8,128)(2,1)S(1)}, u32[]{:S(2)}, u32[]{:S(2)}) collective-permute-start(bf16[128,256]{1,0:T(8,128)(2,1)S(1)} %get-tuple-element.26), channel_id=1, source_target_pairs={{0,4},{4,8},{8,12},{12,16},{16,20},{20,24},{24,28},{1,5},{5,9},{9,... | collective-permute-start | bytes 196616 | tf_op jit(solution)/shard_map/ppermute | solution.py:221
  53.2 11.6 %collective-permute-start.7 = (bf16[128,256]{1,0:T(8,128)(2,1)S(1)}, bf16[128,256]{1,0:T(8,128)(2,1)S(1)}, u32[]{:S(2)}, u32[]{:S(2)}) collective-permute-start(bf16[128,256]{1,0:T(8,128)(2,1)S(1)} %get-tuple-element.27), channel_id=1, source_target_pairs={{4,0},{8,4},{12,8},{16,12},{20,16},{24,20},{28,24},{5,1},{9,5},{13... | collective-permute-start | bytes 196616 | tf_op jit(solution)/shard_map/ppermute | solution.py:221
  74.1 13.1 %copy-start.6 = (s32[1,1,2,2]{3,2,1,0:T(2,128)S(1)}, s32[1,1,2,2]{3,2,1,0:T(2,128)}, u32[]{:S(2)}) copy-start(s32[1,1,2,2]{3,2,1,0:T(2,128)} %param.12) | copy-start | bytes 52
  74.1 13.1 %copy-start.9 = (s32[1,4]{1,0:T(1,128)S(1)}, s32[1,4]{1,0:T(1,128)}, u32[]{:S(2)}) copy-start(s32[1,4]{1,0:T(1,128)} %counts.5) | copy-start | bytes 52
  74.2 9.9 %collective-permute-start.4 = (f32[128,256]{1,0:T(8,128)S(1)}, f32[128,256]{1,0:T(8,128)S(1)}, u32[]{:S(2)}, u32[]{:S(2)}) collective-permute-start(f32[128,256]{1,0:T(8,128)S(1)} %get-tuple-element.32), channel_id=1, source_target_pairs={{0,4},{4,8},{8,12},{12,16},{16,20},{20,24},{24,28},{1,5},{5,9},{9,... | collective-permute-start | bytes 393224 | tf_op jit(solution)/shard_map/ppermute | solution.py:221
  78.8 8.4 %collective-permute-start.5 = (f32[128,256]{1,0:T(8,128)S(1)}, f32[128,256]{1,0:T(8,128)S(1)}, u32[]{:S(2)}, u32[]{:S(2)}) collective-permute-start(f32[128,256]{1,0:T(8,128)S(1)} %get-tuple-element.31), channel_id=1, source_target_pairs={{4,0},{8,4},{12,8},{16,12},{20,16},{24,20},{28,24},{5,1},{9,5},{13... | collective-permute-start | bytes 393224 | tf_op jit(solution)/shard_map/ppermute | solution.py:221
Sparse Core Ops, SparseCore 0:
  74.3 142.2 all-reduce.2

commit v2 on v1

v2 whole, which is shorter than its diff:
```python
import functools

import jax
import jax.numpy as jnp
from jax import lax
from jax.experimental import pallas as pl
from jax.experimental.pallas import tpu as pltpu
from jax.sharding import PartitionSpec as P

F32 = jnp.float32
BF16 = jnp.bfloat16
CHUNK = 256
GROUP = 3
VMEM_LIMIT = 48 * 1024 * 1024


def dot(a, b):
    return jnp.dot(a, b, preferred_element_type=F32)


def dot_nt(a, b):
    return lax.dot_general(a, b, (((1,), (1,)), ((), ())), preferred_element_type=F32)


def dot_tn(a, b):
    return lax.dot_general(a, b, (((0,), (0,)), ((), ())), preferred_element_type=F32)


def one_hot(index_row, count):
    slots = index_row.shape[1]
    index = index_row.astype(F32)
    rows = lax.broadcasted_iota(jnp.int32, (CHUNK, slots), 0).astype(F32).astype(BF16)
    one, zero = jnp.ones((), BF16), jnp.zeros((), BF16)
    parts = []
    for base in range(0, count, CHUNK):
        shifted = jnp.broadcast_to((index - base).astype(BF16), (CHUNK, slots))
        parts.append(jnp.where(rows == shifted, one, zero))
    return jnp.concatenate(parts, axis=0)


def active_mask(counts_ref, blocks, block, width):
    lane = lax.broadcasted_iota(jnp.int32, (width, block), 1)
    return [(lane < counts_ref[0, b]).astype(F32) for b in range(blocks)]


def pick(sends_ref, side, per_side, table, blocks, block):
    picked = []
    for j in range(per_side):
        total = 0.0
        for b in range(blocks):
            total = total + jnp.where(
                sends_ref[side, j] == b, table[:, b * block : (b + 1) * block], 0.0
            )
        picked.append(total)
    return jnp.concatenate(picked, axis=1)


def add_back(own, sends_ref, per_side, from_left, from_right, blocks, block):
    out = []
    for b in range(blocks):
        total = own[:, b * block : (b + 1) * block]
        for side, back in ((0, from_left), (1, from_right)):
            for j in range(per_side):
                total = total + jnp.where(
                    sends_ref[side, j] == b, back[:, j * block : (j + 1) * block], 0.0
                )
        out.append(total)
    return jnp.concatenate(out, axis=1)


class Exchange:
    def __init__(self, topo, local, land, half_own, half_send, land_quad, quad_send, land_line, out, send_sems, recv_sems):
        self.topo, self.local, self.land = topo, local, land
        self.half_own, self.half_send, self.land_quad = half_own, half_send, land_quad
        self.quad_send, self.land_line, self.out = quad_send, land_line, out
        self.send_sems, self.recv_sems = send_sems, recv_sems
        self.half = half_own.shape[0]
        self.quad = self.half // topo.n_quad
        self.piece = self.quad // topo.n_line
        self.next_sem = 0

    def copy(self, src, dst, device):
        sem = self.next_sem
        self.next_sem += 1
        return pltpu.make_async_remote_copy(
            src_ref=src,
            dst_ref=dst,
            send_sem=self.send_sems.at[sem],
            recv_sem=self.recv_sems.at[sem],
            device_id=device,
            device_id_type=pl.DeviceIdType.MESH,
        )

    def start(self, copies):
        for copy in copies:
            copy.start()
        self.flying = copies

    def land_all(self):
        for copy in self.flying:
            copy.wait()

    def stage_core(self):
        t = self.topo
        self.start([
            self.copy(self.local.at[pl.ds((1 - t.core) * self.half, self.half)], self.land, t.device(core=1 - t.core))
        ])

    def stage_quad(self):
        t = self.topo
        self.land_all()
        total = self.local[pl.ds(t.core * self.half, self.half)] + self.land[...]
        self.half_own[...] = total
        self.half_send[...] = total.astype(BF16)
        copies = []
        for d in range(1, t.n_quad):
            q = lax.rem(t.quad + d, t.n_quad)
            copies.append(self.copy(
                self.half_send.at[pl.ds(q * self.quad, self.quad)], self.land_quad.at[d - 1], t.device(quad=q)
            ))
        self.start(copies)

    def stage_line(self):
        t = self.topo
        self.land_all()
        total = self.half_own[pl.ds(t.quad * self.quad, self.quad)]
        for d in range(1, t.n_quad):
            total = total + self.land_quad[d - 1].astype(F32)
        self.half_own[pl.ds(t.quad * self.quad, self.quad)] = total
        self.quad_send[...] = total.astype(BF16)
        copies = []
        for d in range(1, t.n_line):
            w = lax.rem(t.line + d, t.n_line)
            copies.append(self.copy(
                self.quad_send.at[pl.ds(w * self.piece, self.piece)], self.land_line.at[d - 1], t.device(line=w)
            ))
        self.start(copies)

    def stage_share_line(self):
        t = self.topo
        self.land_all()
        total = self.half_own[pl.ds(t.quad * self.quad + t.line * self.piece, self.piece)]
        for d in range(1, t.n_line):
            total = total + self.land_line[d - 1].astype(F32)
        place = pl.ds(t.core * self.half + t.quad * self.quad + t.line * self.piece, self.piece)
        self.out[place] = total.astype(BF16)
        self.start([
            self.copy(self.out.at[place], self.out.at[place], t.device(line=lax.rem(t.line + d, t.n_line)))
            for d in range(1, t.n_line)
        ])

    def stage_share_quad(self):
        t = self.topo
        self.land_all()
        place = pl.ds(t.core * self.half + t.quad * self.quad, self.quad)
        self.start([
            self.copy(self.out.at[place], self.out.at[place], t.device(quad=lax.rem(t.quad + d, t.n_quad)))
            for d in range(1, t.n_quad)
        ])

    def stage_share_core(self):
        t = self.topo
        self.land_all()
        place = pl.ds(t.core * self.half, self.half)
        self.start([self.copy(self.out.at[place], self.out.at[place], t.device(core=1 - t.core))])


class Topology:
    def __init__(self, n_space, n_dp):
        self.n_space, self.n_dp = n_space, n_dp
        self.n_line = n_space // 2
        self.n_quad = (n_dp // 2) * 2
        self.space, self.dp = lax.axis_index("space"), lax.axis_index("dp")
        self.core = lax.rem(self.dp, 2)
        self.quad = (self.dp // 2) * 2 + lax.rem(self.space, 2)
        self.line = self.space // 2

    def device(self, core=None, quad=None, line=None):
        core = self.core if core is None else core
        quad = self.quad if quad is None else quad
        line = self.line if line is None else line
        return (line * 2 + lax.rem(quad, 2), (quad // 2) * 2 + core)

    def partners(self):
        found = [self.device(core=1 - self.core)]
        found += [self.device(quad=lax.rem(self.quad + d, self.n_quad)) for d in range(1, self.n_quad)]
        found += [self.device(line=lax.rem(self.line + d, self.n_line)) for d in range(1, self.n_line)]
        found += [(lax.rem(self.space + d, self.n_space), self.dp) for d in (1, self.n_space - 1)]
        return found


def exchange_copies(n_quad, n_line):
    return 2 * (1 + (n_quad - 1) + (n_line - 1))


def whole_kernel(
    dims, n_space, n_dp,
    feats, cot, weight_one, weight_two, rules, sends, counts,
    grad_rows, out_one, out_two,
    xa_t, ga_t, gga, gx, prod, ext, z, slope, dz, dext, dext_rim, rim_low, rim_high, rim32, halo_bf, halo_f32,
    local_one, local_two, land, half_own, half_send, land_quad, quad_send, land_line,
    send_sems, recv_sems, halo_send_sems, halo_recv_sems,
):
    blocks, block, per_side = dims
    rows, width = feats.shape
    halo = per_side * block
    ext_rows = rows + 2 * halo
    kernels, slots = rules.shape[1:]
    groups = kernels // GROUP
    topo = Topology(n_space, n_dp)
    barrier = pltpu.get_barrier_semaphore()
    partners = topo.partners()
    for device in partners:
        pl.semaphore_signal(barrier, inc=1, device_id=device, device_id_type=pl.DeviceIdType.MESH)

    mask = jnp.concatenate(active_mask(counts, blocks, block, width), axis=1)
    xa = feats[...].astype(F32).T * mask
    xa_t[...] = xa.astype(BF16)
    ga_t[...] = (cot[...].astype(F32).T * mask).astype(BF16)
    rim_low[0] = pick(sends, 0, per_side, xa, blocks, block).astype(BF16)
    rim_high[0] = pick(sends, 1, per_side, xa, blocks, block).astype(BF16)
    for s in range(2):
        @pl.when(topo.space == 0)
        def _():
            halo_bf[s, 0] = jnp.zeros((width, halo), BF16)
            halo_f32[s, 0] = jnp.zeros((width, halo), F32)

        @pl.when(topo.space == n_space - 1)
        def _():
            halo_bf[s, 1] = jnp.zeros((width, halo), BF16)
            halo_f32[s, 1] = jnp.zeros((width, halo), F32)

    per = width // 16
    pad = (local_one.shape[0] // per) - kernels
    for local in (local_one, local_two):
        if pad:
            local[pl.ds(kernels * per, pad * per)] = jnp.zeros((pad * per, 16, width), F32)
    pl.semaphore_wait(barrier, len(partners))

    def halo_copies(which, to_low, to_high, landing):
        def make(src, side, device):
            return pltpu.make_async_remote_copy(
                src_ref=src,
                dst_ref=landing.at[side],
                send_sem=halo_send_sems.at[which, side],
                recv_sem=halo_recv_sems.at[which, side],
                device_id=(device, topo.dp),
                device_id_type=pl.DeviceIdType.MESH,
            )
        up = make(to_high, 0, lax.rem(topo.space + 1, n_space))
        down = make(to_low, 1, lax.rem(topo.space + n_space - 1, n_space))
        return up, down

    def halo_start(copies):
        up, down = copies

        @pl.when(topo.space < n_space - 1)
        def _():
            up.start()

        @pl.when(topo.space > 0)
        def _():
            down.start()

    def halo_wait(copies):
        up, down = copies

        @pl.when(topo.space < n_space - 1)
        def _():
            up.wait_send()
            down.wait_recv()

        @pl.when(topo.space > 0)
        def _():
            down.wait_send()
            up.wait_recv()

    x_copies = halo_copies(0, rim_low.at[0], rim_high.at[0], halo_bf.at[0])
    halo_start(x_copies)

    dext[...] = jnp.zeros_like(dext)

    def back_two(i, _):
        weights, placed = [], []
        for j in range(GROUP):
            k = i * GROUP + j
            gathered = dot(ga_t[...], one_hot(rules[1, pl.ds(k, 1), :], rows)).astype(BF16)
            gga[k] = gathered
            placed.append(
                dot_nt(gathered, one_hot(rules[0, pl.ds(k, 1), :], ext_rows)).astype(BF16)
            )
            weights.append(weight_two[k])
        dext[...] += dot(jnp.concatenate(weights, axis=1), jnp.concatenate(placed, axis=0))
        return 0

    lax.fori_loop(0, groups, back_two, 0)
    dext_rim[0, 0] = dext[:, rows : rows + halo]
    dext_rim[0, 1] = dext[:, rows + halo :]
    dy_copies = halo_copies(1, dext_rim.at[0, 0], dext_rim.at[0, 1], halo_f32.at[0])
    halo_start(dy_copies)

    halo_wait(x_copies)
    ext[:, :rows] = xa_t[...]
    ext[:, rows : rows + halo] = halo_bf[0, 0]
    ext[:, rows + halo :] = halo_bf[0, 1]
    z[...] = jnp.zeros_like(z)

    def forward(i, _):
        weights, placed = [], []
        for j in range(GROUP):
            k = i * GROUP + j
            gathered = dot(ext[...], one_hot(rules[0, pl.ds(k, 1), :], ext_rows)).astype(BF16)
            gx[k] = gathered
            placed.append(dot_nt(gathered, one_hot(rules[1, pl.ds(k, 1), :], rows)).astype(BF16))
            weights.append(weight_one[k])
        z[...] += dot_tn(jnp.concatenate(weights, axis=0), jnp.concatenate(placed, axis=0))
        return 0

    lax.fori_loop(0, groups, forward, 0)
    zv = z[...]
    sig = 1.0 / (1.0 + jnp.exp(-zv))
    y = ((zv * sig) * mask).astype(BF16)
    slope[...] = sig * (1.0 + zv * (1.0 - sig)) * mask
    y32 = y.astype(F32)
    rim_low[1] = pick(sends, 0, per_side, y32, blocks, block).astype(BF16)
    rim_high[1] = pick(sends, 1, per_side, y32, blocks, block).astype(BF16)
    y_copies = halo_copies(2, rim_low.at[1], rim_high.at[1], halo_bf.at[1])
    halo_start(y_copies)
    ext[:, :rows] = y

    halo_wait(dy_copies)
    dy = add_back(
        dext[:, :rows], sends, per_side, halo_f32[0, 0], halo_f32[0, 1], blocks, block
    )
    dz[...] = (dy * slope[...]).astype(BF16)

    def grad_first(i, _):
        for j in range(GROUP):
            k = i * GROUP + j
            gathered = dot(dz[...], one_hot(rules[1, pl.ds(k, 1), :], rows)).astype(BF16)
            local_one[pl.ds(k * per, per)] = dot_nt(gx[k], gathered).reshape(per, 16, width)
            prod[k] = dot(weight_one[k], gathered).astype(BF16)
        return 0

    lax.fori_loop(0, groups, grad_first, 0)

    def exchange(side, local, out):
        return Exchange(
            topo, local, land.at[side], half_own.at[side], half_send.at[side], land_quad.at[side],
            quad_send.at[side], land_line.at[side], out, send_sems.at[side], recv_sems.at[side],
        )

    one = exchange(0, local_one, out_one)
    two = exchange(1, local_two, out_two)
    one.stage_core()

    halo_wait(y_copies)
    ext[:, rows : rows + halo] = halo_bf[1, 0]
    ext[:, rows + halo :] = halo_bf[1, 1]

    def grad_second(i, _):
        for j in range(GROUP):
            k = i * GROUP + j
            gathered = dot(ext[...], one_hot(rules[0, pl.ds(k, 1), :], ext_rows)).astype(BF16)
            local_two[pl.ds(k * per, per)] = dot_nt(gathered, gga[k]).reshape(per, 16, width)
        return 0

    cut = (2 * groups) // 3
    lax.fori_loop(0, cut, grad_second, 0)
    one.stage_quad()
    lax.fori_loop(cut, groups, grad_second, 0)
    two.stage_core()

    dext[...] = jnp.zeros_like(dext)

    def back_one(i, _):
        products, selectors = [], []
        for j in range(GROUP):
            k = i * GROUP + j
            products.append(prod[k])
            selectors.append(one_hot(rules[0, pl.ds(k, 1), :], ext_rows))
        dext[...] += dot_nt(jnp.concatenate(products, axis=1), jnp.concatenate(selectors, axis=1))
        return 0

    cut_a, cut_b = groups // 3, (2 * groups) // 3
    lax.fori_loop(0, cut_a, back_one, 0)
    two.stage_quad()
    one.stage_line()
    lax.fori_loop(cut_a, cut_b, back_one, 0)
    one.stage_share_line()
    lax.fori_loop(cut_b, groups, back_one, 0)
    dext_rim[1, 0] = dext[:, rows : rows + halo]
    dext_rim[1, 1] = dext[:, rows + halo :]
    dx_copies = halo_copies(3, dext_rim.at[1, 0], dext_rim.at[1, 1], halo_f32.at[1])
    halo_start(dx_copies)
    two.stage_line()
    one.stage_share_quad()
    halo_wait(dx_copies)
    own = add_back(
        dext[:, :rows], sends, per_side, halo_f32[1, 0], halo_f32[1, 1], blocks, block
    )
    grad_rows[...] = (own * mask).T
    two.stage_share_line()
    one.stage_share_core()
    two.stage_share_quad()
    one.land_all()
    two.stage_share_core()
    two.land_all()


def body(n_space, n_dp, features, cotangent, weight_one, weight_two, rules, halo_send, block_counts):
    feats, cot, links, sends = features[0], cotangent[0], rules[0, 0], halo_send[0, 0]
    rows, width = feats.shape
    blocks = block_counts.shape[1]
    block = rows // blocks
    per_side = sends.shape[1]
    halo = per_side * block
    kernels, slots = links.shape[1:]
    ext_rows = rows + 2 * halo
    per = width // 16
    devices = n_space * n_dp
    padded = kernels
    while (padded * per) % devices:
        padded += 1
    tiles = padded * per
    half = tiles // 2
    n_quad, n_line = (n_dp // 2) * 2, n_space // 2
    quad = half // n_quad
    piece = quad // n_line
    copies = exchange_copies(n_quad, n_line)
    v, s = pltpu.VMEM, pltpu.SMEM
    grad_rows, one, two = pl.pallas_call(
        functools.partial(whole_kernel, (blocks, block, per_side), n_space, n_dp),
        out_shape=[
            jax.ShapeDtypeStruct((rows, width), F32),
            jax.ShapeDtypeStruct((tiles, 16, width), BF16),
            jax.ShapeDtypeStruct((tiles, 16, width), BF16),
        ],
        in_specs=[pl.BlockSpec(memory_space=m) for m in (v, v, v, v, v, s, s)],
        out_specs=[pl.BlockSpec(memory_space=v)] * 3,
        scratch_shapes=[
            v((width, rows), BF16),
            v((width, rows), BF16),
            v((kernels, width, slots), BF16),
            v((kernels, width, slots), BF16),
            v((kernels, width, slots), BF16),
            v((width, ext_rows), BF16),
            v((width, rows), F32),
            v((width, rows), F32),
            v((width, rows), BF16),
            v((width, ext_rows), F32),
            v((2, 2, width, halo), F32),
            v((2, width, halo), BF16),
            v((2, width, halo), BF16),
            v((8, 128), F32),
            v((2, 2, width, halo), BF16),
            v((2, 2, width, halo), F32),
            v((tiles, 16, width), F32),
            v((tiles, 16, width), F32),
            v((2, half, 16, width), F32),
            v((2, half, 16, width), F32),
            v((2, half, 16, width), BF16),
            v((2, n_quad - 1, quad, 16, width), BF16),
            v((2, quad, 16, width), BF16),
            v((2, n_line - 1, piece, 16, width), BF16),
            pltpu.SemaphoreType.DMA((2, copies)),
            pltpu.SemaphoreType.DMA((2, copies)),
            pltpu.SemaphoreType.DMA((4, 2)),
            pltpu.SemaphoreType.DMA((4, 2)),
        ],
        compiler_params=pltpu.CompilerParams(
            collective_id=0, has_side_effects=True, vmem_limit_bytes=VMEM_LIMIT
        ),
    )(feats, cot, weight_one, weight_two, links, sends, block_counts)
    scale = 1.0 / jnp.sqrt(F32(devices * slots))

    def finish(total):
        return total[: kernels * per].astype(F32).reshape(kernels, width, width) * scale

    return (grad_rows[None], finish(one), finish(two))


def solution(mesh):
    n_space, n_dp = mesh.shape["space"], mesh.shape["dp"]
    in_specs = (
        P("dp", "space", None),
        P("dp", "space", None),
        P(),
        P(),
        P("dp", "space", None, None, None),
        P("dp", "space", None, None),
        P("dp", "space"),
    )
    out_specs = (P("dp", "space", None), P(), P())
    return jax.shard_map(
        functools.partial(body, n_space, n_dp), mesh=mesh, in_specs=in_specs, out_specs=out_specs, check_vma=False)
```

time: 228 us -> 78.2 us (0.34)
  waiting for transfers between devices: 139 us -> 0 us
  Pallas kernels: 41.3 us -> 68.1 us
  starting transfers between devices: 22.2 us -> 0 us
  between operations: 14.2 us -> 0.65 us
  other arithmetic: 4.39 us -> 2.1 us
    psum x1 -> x0, waiting for transfers between devices: 128 us -> none  [body(): total_one = lax.psum(grad_one, ('space', 'dp'))]
    pallas_call x6 -> x1, Pallas kernels: 41.3 us -> 68.1 us  [body(): pl.pallas_call(functools.partial(whole_kernel, (blocks, block, per_side),...]
    ppermute x8 -> x0, starting transfers between devices: 22.2 us -> none  [the longest x4 17 us: swap(): lax.ppermute(to_high, 'space', up)]
    ppermute x8 -> x0, waiting for transfers between devices: 11.2 us -> none  [the longest x4 7.14 us: swap(): lax.ppermute(to_low, 'space', down)]
    mul x1, other arithmetic: 4.39 us -> 2.1 us  [finish(): total[:kernels * per].astype(F32).reshape(kernels, width, width) * scale]
    unnamed x21 -> x14, local copies, waits for them, and re-layouts: 6.54 us -> 7 us
  transfers between devices with their start and end apart: 9 -> 0, of which waited for: 4 -> 0; matrix products, arithmetic and copies ran while one was open for 0% -> 0% of each run, Pallas kernels for 9% -> 0%
where the time goes in v2:
time: 78.2 us; the launch traced here: 77.9 us
  Pallas kernels  68.1 us (87%)
  local copies, waits for them, and re-layouts  7 us (9%)
  other arithmetic  2.1 us (3%)
    pallas_call x1, Pallas kernels, body(): pl.pallas_call(functools.partial(whole_kernel, (blocks, block, per_side),...  68.1 us
    unnamed x14, local copies, waits for them, and re-layouts  7 us
    mul x1, other arithmetic, finish(): total[:kernels * per].astype(F32).reshape(kernels, width, width) * scale  2.1 us

profile of v2, /device:TPU:0, one launch (start us, length us, event | category | flops | bytes accessed | tf_op | source)
XLA Modules:
  0.0 77.9 jit_solution(13408295293745941650)
XLA Ops:
  0.6 0.8 %copy.12 = s32[1,1,2,27,256]{4,3,2,1,0:T(8,128)S(1)} copy(s32[1,1,2,27,256]{4,2,3,1,0:T(2,128)} %param.11) | data formatting | bytes 110592 | tf_op args[4]
  1.5 0.0 copy-start
  1.5 1.2 %copy-done = bf16[27,128,128]{2,1,0:T(8,128)(2,1)S(1)} copy-done((bf16[27,128,128]{2,1,0:T(8,128)(2,1)S(1)}, bf16[27,128,128]{2,1,0:T(8,128)(2,1)}, u32[]{:S(2)}) %copy-start) | copy-done | bytes 884760
  2.6 0.0 copy-start.1
  2.6 1.2 %copy-done.1 = bf16[27,128,128]{2,1,0:T(8,128)(2,1)S(1)} copy-done((bf16[27,128,128]{2,1,0:T(8,128)(2,1)S(1)}, bf16[27,128,128]{2,1,0:T(8,128)(2,1)}, u32[]{:S(2)}) %copy-start.1) | copy-done | bytes 884760
  3.8 0.0 copy-start.2
  3.8 0.9 %copy-done.2 = bf16[1,512,128]{2,1,0:T(8,128)(2,1)S(1)} copy-done((bf16[1,512,128]{2,1,0:T(8,128)(2,1)S(1)}, bf16[1,512,128]{2,1,0:T(8,128)(2,1)}, u32[]{:S(2)}) %copy-start.2) | copy-done | bytes 131096
  4.7 0.0 copy-start.3
  4.7 0.9 %copy-done.3 = bf16[1,512,128]{2,1,0:T(8,128)(2,1)S(1)} copy-done((bf16[1,512,128]{2,1,0:T(8,128)(2,1)S(1)}, bf16[1,512,128]{2,1,0:T(8,128)(2,1)}, u32[]{:S(2)}) %copy-start.3) | copy-done | bytes 131096
  5.6 0.0 copy-start.4
  5.6 0.7 copy-done.4
  6.3 0.0 copy-start.5
  6.3 0.7 copy-done.5
  6.9 68.1 %shard_map.94 = (f32[512,128]{1,0:T(8,128)S(1)}, bf16[224,16,128]{2,1,0:T(8,128)(2,1)S(1)}, bf16[224,16,128]{2,1,0:T(8,128)(2,1)S(1)}) custom-call(bf16[512,128]{1,0:T(8,128)(2,1)S(1)} %bitcast.11, bf16[512,128]{1,0:T(8,128)(2,1)S(1)} %bitcast.12, bf16[27,128,128]{2,1,0:T(8,128)(2,1)S(1)} %copy-done, bf16[27,128,128]{2,1,0:T(8,128)(2,1)S(1)} %copy-done.1, ...), custom_call_target="tpu_custom_call" | custom-call | tf_op jit(solution)/shard_map/pallas_call | solution.py:432
  75.1 2.1 %convert_multiply_fusion = (f32[216,16,128]{2,1,0:T(8,128)}, f32[216,16,128]{2,1,0:T(8,128)}) fusion(bf16[224,16,128]{2,1,0:T(8,128)(2,1)S(1)} %get-tuple-element.8, bf16[224,16,128]{2,1,0:T(8,128)(2,1)S(1)} %get-tuple-element.7), kind=kLoop, calls=%fused_computation | loop fusion | flops 1769472 | bytes 5308416 | tf_op jit(solution)/shard_map/mul | solution.py:478
  77.2 0.7 copy.14
Async XLA Ops:
  1.5 1.2 %copy-start = (bf16[27,128,128]{2,1,0:T(8,128)(2,1)S(1)}, bf16[27,128,128]{2,1,0:T(8,128)(2,1)}, u32[]{:S(2)}) copy-start(bf16[27,128,128]{2,1,0:T(8,128)(2,1)} %weight_one.1) | copy-start | bytes 2654212
  2.6 1.2 %copy-start.1 = (bf16[27,128,128]{2,1,0:T(8,128)(2,1)S(1)}, bf16[27,128,128]{2,1,0:T(8,128)(2,1)}, u32[]{:S(2)}) copy-start(bf16[27,128,128]{2,1,0:T(8,128)(2,1)} %weight_two.1) | copy-start | bytes 2654212
  3.8 0.9 %copy-start.2 = (bf16[1,512,128]{2,1,0:T(8,128)(2,1)S(1)}, bf16[1,512,128]{2,1,0:T(8,128)(2,1)}, u32[]{:S(2)}) copy-start(bf16[1,512,128]{2,1,0:T(8,128)(2,1)} %param.7) | copy-start | bytes 393220
  4.7 0.9 %copy-start.3 = (bf16[1,512,128]{2,1,0:T(8,128)(2,1)S(1)}, bf16[1,512,128]{2,1,0:T(8,128)(2,1)}, u32[]{:S(2)}) copy-start(bf16[1,512,128]{2,1,0:T(8,128)(2,1)} %param.8) | copy-start | bytes 393220
  5.6 0.7 copy-start.4
  6.3 0.7 copy-start.5

commit v3 on v2

--- a/solution.py
+++ b/solution.py
@@ -26,16 +26,43 @@
     return lax.dot_general(a, b, (((0,), (0,)), ((), ())), preferred_element_type=F32)
 
 
-def one_hot(index_row, count):
-    slots = index_row.shape[1]
-    index = index_row.astype(F32)
-    rows = lax.broadcasted_iota(jnp.int32, (CHUNK, slots), 0).astype(F32).astype(BF16)
-    one, zero = jnp.ones((), BF16), jnp.zeros((), BF16)
-    parts = []
-    for base in range(0, count, CHUNK):
-        shifted = jnp.broadcast_to((index - base).astype(BF16), (CHUNK, slots))
-        parts.append(jnp.where(rows == shifted, one, zero))
-    return jnp.concatenate(parts, axis=0)
+def one_hot(low_row):
+    slots = low_row.shape[1]
+    place = lax.broadcasted_iota(jnp.int32, (CHUNK, slots), 0).astype(F32).astype(BF16)
+    return jnp.where(
+        place == jnp.broadcast_to(low_row.astype(BF16), (CHUNK, slots)),
+        jnp.ones((), BF16), jnp.zeros((), BF16),
+    )
+
+
+def gather(table, selector, chunk_row, width):
+    found = dot(table, selector)
+    chunks = table.shape[0] // width
+    chunk = jnp.broadcast_to(chunk_row, (width, chunk_row.shape[1]))
+    out = found[:width]
+    for c in range(1, chunks):
+        out = jnp.where(chunk == c, found[c * width : (c + 1) * width], out)
+    return out.astype(BF16)
+
+
+def spread(values, chunk_row, chunks):
+    chunk = jnp.broadcast_to(chunk_row.astype(BF16), values.shape)
+    zero = jnp.zeros((), BF16)
+    return jnp.concatenate(
+        [jnp.where(chunk == jnp.asarray(c, BF16), values, zero) for c in range(chunks)], axis=0
+    )
+
+
+def stack(table):
+    return jnp.concatenate(
+        [table[:, c : c + CHUNK] for c in range(0, table.shape[1], CHUNK)], axis=0
+    )
+
+
+def unstack(table, width):
+    return jnp.concatenate(
+        [table[r : r + width] for r in range(0, table.shape[0], width)], axis=1
+    )
 
 
 def active_mask(counts_ref, blocks, block, width):
@@ -197,7 +224,7 @@
     dims, n_space, n_dp,
     feats, cot, weight_one, weight_two, rules, sends, counts,
     grad_rows, out_one, out_two,
-    xa_t, ga_t, gga, gx, prod, ext, z, slope, dz, dext, dext_rim, rim_low, rim_high, rim32, halo_bf, halo_f32,
+    xa_t, ga_t, gga, gx, prod, ext, z, slope, dz, dext, dext_rim, rim_low, rim_high, rim32, halo_bf, halo_f32, low_rows, chunk_rows,
     local_one, local_two, land, half_own, half_send, land_quad, quad_send, land_line,
     send_sems, recv_sems, halo_send_sems, halo_recv_sems,
 ):
@@ -207,6 +234,25 @@
     ext_rows = rows + 2 * halo
     kernels, slots = rules.shape[1:]
     groups = kernels // GROUP
+    own_chunks, ext_chunks = rows // CHUNK, ext_rows // CHUNK
+
+    def selector(kind, k):
+        return one_hot(low_rows[kind, pl.ds(k, 1), :])
+
+    def chunk_of(kind, k):
+        return chunk_rows[kind, pl.ds(k, 1), :]
+
+    def own_part(ref):
+        return unstack(ref[pl.ds(0, own_chunks * width)], width)
+
+    def rim_part(ref, side):
+        size = (halo // CHUNK) * width
+        return unstack(ref[pl.ds(own_chunks * width + side * size, size)], width)
+
+    def set_rim(ref, side, value):
+        size = (halo // CHUNK) * width
+        ref[pl.ds(own_chunks * width + side * size, size)] = stack(value)
+
     topo = Topology(n_space, n_dp)
     barrier = pltpu.get_barrier_semaphore()
     partners = topo.partners()
@@ -214,9 +260,13 @@
         pl.semaphore_signal(barrier, inc=1, device_id=device, device_id_type=pl.DeviceIdType.MESH)
 
     mask = jnp.concatenate(active_mask(counts, blocks, block, width), axis=1)
+    for kind, limit in ((0, ext_rows), (1, rows)):
+        index = rules[kind]
+        low_rows[kind] = jnp.where(index < limit, lax.rem(index, CHUNK), -1).astype(F32)
+        chunk_rows[kind] = (index // CHUNK).astype(F32)
     xa = feats[...].astype(F32).T * mask
-    xa_t[...] = xa.astype(BF16)
-    ga_t[...] = (cot[...].astype(F32).T * mask).astype(BF16)
+    xa_t[...] = stack(xa.astype(BF16))
+    ga_t[...] = stack((cot[...].astype(F32).T * mask).astype(BF16))
     rim_low[0] = pick(sends, 0, per_side, xa, blocks, block).astype(BF16)
     rim_high[0] = pick(sends, 1, per_side, xa, blocks, block).astype(BF16)
     for s in range(2):
@@ -284,40 +334,48 @@
         weights, placed = [], []
         for j in range(GROUP):
             k = i * GROUP + j
-            gathered = dot(ga_t[...], one_hot(rules[1, pl.ds(k, 1), :], rows)).astype(BF16)
-            gga[k] = gathered
+            found = gather(ga_t[...], selector(1, k), chunk_of(1, k), width)
+            gga[k] = found
             placed.append(
-                dot_nt(gathered, one_hot(rules[0, pl.ds(k, 1), :], ext_rows)).astype(BF16)
+                dot_nt(spread(found, chunk_of(0, k), ext_chunks), selector(0, k)).astype(BF16)
             )
             weights.append(weight_two[k])
-        dext[...] += dot(jnp.concatenate(weights, axis=1), jnp.concatenate(placed, axis=0))
+        weights = jnp.concatenate(weights, axis=1)
+        for c in range(ext_chunks):
+            part = slice(c * width, (c + 1) * width)
+            dext[part] += dot(weights, jnp.concatenate([p[part] for p in placed], axis=0))
         return 0
 
     lax.fori_loop(0, groups, back_two, 0)
-    dext_rim[0, 0] = dext[:, rows : rows + halo]
-    dext_rim[0, 1] = dext[:, rows + halo :]
+    dext_rim[0, 0] = rim_part(dext, 0)
+    dext_rim[0, 1] = rim_part(dext, 1)
     dy_copies = halo_copies(1, dext_rim.at[0, 0], dext_rim.at[0, 1], halo_f32.at[0])
     halo_start(dy_copies)
 
     halo_wait(x_copies)
-    ext[:, :rows] = xa_t[...]
-    ext[:, rows : rows + halo] = halo_bf[0, 0]
-    ext[:, rows + halo :] = halo_bf[0, 1]
+    ext[pl.ds(0, own_chunks * width)] = xa_t[...]
+    set_rim(ext, 0, halo_bf[0, 0])
+    set_rim(ext, 1, halo_bf[0, 1])
     z[...] = jnp.zeros_like(z)
 
     def forward(i, _):
         weights, placed = [], []
         for j in range(GROUP):
             k = i * GROUP + j
-            gathered = dot(ext[...], one_hot(rules[0, pl.ds(k, 1), :], ext_rows)).astype(BF16)
-            gx[k] = gathered
-            placed.append(dot_nt(gathered, one_hot(rules[1, pl.ds(k, 1), :], rows)).astype(BF16))
+            found = gather(ext[...], selector(0, k), chunk_of(0, k), width)
+            gx[k] = found
+            placed.append(
+                dot_nt(spread(found, chunk_of(1, k), own_chunks), selector(1, k)).astype(BF16)
+            )
             weights.append(weight_one[k])
-        z[...] += dot_tn(jnp.concatenate(weights, axis=0), jnp.concatenate(placed, axis=0))
+        weights = jnp.concatenate(weights, axis=0)
+        for c in range(own_chunks):
+            part = slice(c * width, (c + 1) * width)
+            z[part] += dot_tn(weights, jnp.concatenate([p[part] for p in placed], axis=0))
         return 0
 
     lax.fori_loop(0, groups, forward, 0)
-    zv = z[...]
+    zv = unstack(z[...], width)
     sig = 1.0 / (1.0 + jnp.exp(-zv))
     y = ((zv * sig) * mask).astype(BF16)
     slope[...] = sig * (1.0 + zv * (1.0 - sig)) * mask
@@ -326,18 +384,18 @@
     rim_high[1] = pick(sends, 1, per_side, y32, blocks, block).astype(BF16)
     y_copies = halo_copies(2, rim_low.at[1], rim_high.at[1], halo_bf.at[1])
     halo_start(y_copies)
-    ext[:, :rows] = y
+    ext[pl.ds(0, own_chunks * width)] = stack(y)
 
     halo_wait(dy_copies)
     dy = add_back(
-        dext[:, :rows], sends, per_side, halo_f32[0, 0], halo_f32[0, 1], blocks, block
-    )
-    dz[...] = (dy * slope[...]).astype(BF16)
+        own_part(dext), sends, per_side, halo_f32[0, 0], halo_f32[0, 1], blocks, block
+    )
+    dz[...] = stack((dy * slope[...]).astype(BF16))
 
     def grad_first(i, _):
         for j in range(GROUP):
             k = i * GROUP + j
-            gathered = dot(dz[...], one_hot(rules[1, pl.ds(k, 1), :], rows)).astype(BF16)
+            gathered = gather(dz[...], selector(1, k), chunk_of(1, k), width)
             local_one[pl.ds(k * per, per)] = dot_nt(gx[k], gathered).reshape(per, 16, width)
             prod[k] = dot(weight_one[k], gathered).astype(BF16)
         return 0
@@ -355,13 +413,13 @@
     one.stage_core()
 
     halo_wait(y_copies)
-    ext[:, rows : rows + halo] = halo_bf[1, 0]
-    ext[:, rows + halo :] = halo_bf[1, 1]
+    set_rim(ext, 0, halo_bf[1, 0])
+    set_rim(ext, 1, halo_bf[1, 1])
 
     def grad_second(i, _):
         for j in range(GROUP):
             k = i * GROUP + j
-            gathered = dot(ext[...], one_hot(rules[0, pl.ds(k, 1), :], ext_rows)).astype(BF16)
+            gathered = gather(ext[...], selector(0, k), chunk_of(0, k), width)
             local_two[pl.ds(k * per, per)] = dot_nt(gathered, gga[k]).reshape(per, 16, width)
         return 0
 
@@ -377,8 +435,8 @@
         products, selectors = [], []
         for j in range(GROUP):
             k = i * GROUP + j
-            products.append(prod[k])
-            selectors.append(one_hot(rules[0, pl.ds(k, 1), :], ext_rows))
+            products.append(spread(prod[k], chunk_of(0, k), ext_chunks))
+            selectors.append(selector(0, k))
         dext[...] += dot_nt(jnp.concatenate(products, axis=1), jnp.concatenate(selectors, axis=1))
         return 0
 
@@ -389,15 +447,15 @@
     lax.fori_loop(cut_a, cut_b, back_one, 0)
     one.stage_share_line()
     lax.fori_loop(cut_b, groups, back_one, 0)
-    dext_rim[1, 0] = dext[:, rows : rows + halo]
-    dext_rim[1, 1] = dext[:, rows + halo :]
+    dext_rim[1, 0] = rim_part(dext, 0)
+    dext_rim[1, 1] = rim_part(dext, 1)
     dx_copies = halo_copies(3, dext_rim.at[1, 0], dext_rim.at[1, 1], halo_f32.at[1])
     halo_start(dx_copies)
     two.stage_line()
     one.stage_share_quad()
     halo_wait(dx_copies)
     own = add_back(
-        dext[:, :rows], sends, per_side, halo_f32[1, 0], halo_f32[1, 1], blocks, block
+        own_part(dext), sends, per_side, halo_f32[1, 0], halo_f32[1, 1], blocks, block
     )
     grad_rows[...] = (own * mask).T
     two.stage_share_line()
@@ -439,22 +497,24 @@
         in_specs=[pl.BlockSpec(memory_space=m) for m in (v, v, v, v, v, s, s)],
         out_specs=[pl.BlockSpec(memory_space=v)] * 3,
         scratch_shapes=[
-            v((width, rows), BF16),
-            v((width, rows), BF16),
+            v((width * rows // CHUNK, CHUNK), BF16),
+            v((width * rows // CHUNK, CHUNK), BF16),
             v((kernels, width, slots), BF16),
             v((kernels, width, slots), BF16),
             v((kernels, width, slots), BF16),
-            v((width, ext_rows), BF16),
+            v((width * ext_rows // CHUNK, CHUNK), BF16),
+            v((width * rows // CHUNK, CHUNK), F32),
             v((width, rows), F32),
-            v((width, rows), F32),
-            v((width, rows), BF16),
-            v((width, ext_rows), F32),
+            v((width * rows // CHUNK, CHUNK), BF16),
+            v((width * ext_rows // CHUNK, CHUNK), F32),
             v((2, 2, width, halo), F32),
             v((2, width, halo), BF16),
             v((2, width, halo), BF16),
             v((8, 128), F32),
             v((2, 2, width, halo), BF16),
             v((2, 2, width, halo), F32),
+            v((2, kernels, slots), F32),
+            v((2, kernels, slots), F32),
             v((tiles, 16, width), F32),
             v((tiles, 16, width), F32),
             v((2, half, 16, width), F32),

time: 78.2 us -> 78.4 us (level)
  no operation moved by 1% of the time
where the time goes in v3:
time: 78.4 us; the launch traced here: 78.1 us
  Pallas kernels  68.3 us (87%)
  local copies, waits for them, and re-layouts  7 us (9%)
  other arithmetic  2.1 us (3%)
    pallas_call x1, Pallas kernels, body(): pl.pallas_call(functools.partial(whole_kernel, (blocks, block, per_side),...  68.3 us
    unnamed x14, local copies, waits for them, and re-layouts  7 us
    mul x1, other arithmetic, finish(): total[:kernels * per].astype(F32).reshape(kernels, width, width) * scale  2.1 us

profile of v3, /device:TPU:0, one launch (start us, length us, event | category | flops | bytes accessed | tf_op | source)
XLA Modules:
  0.0 78.1 jit_solution(10339827809313590182)
XLA Ops:
  0.6 0.8 %copy.12 = s32[1,1,2,27,256]{4,3,2,1,0:T(8,128)S(1)} copy(s32[1,1,2,27,256]{4,2,3,1,0:T(2,128)} %param.11) | data formatting | bytes 110592 | tf_op args[4]
  1.5 0.0 copy-start
  1.5 1.2 %copy-done = bf16[27,128,128]{2,1,0:T(8,128)(2,1)S(1)} copy-done((bf16[27,128,128]{2,1,0:T(8,128)(2,1)S(1)}, bf16[27,128,128]{2,1,0:T(8,128)(2,1)}, u32[]{:S(2)}) %copy-start) | copy-done | bytes 884760
  2.6 0.0 copy-start.1
  2.6 1.2 %copy-done.1 = bf16[27,128,128]{2,1,0:T(8,128)(2,1)S(1)} copy-done((bf16[27,128,128]{2,1,0:T(8,128)(2,1)S(1)}, bf16[27,128,128]{2,1,0:T(8,128)(2,1)}, u32[]{:S(2)}) %copy-start.1) | copy-done | bytes 884760
  3.8 0.0 copy-start.2
  3.8 0.9 %copy-done.2 = bf16[1,512,128]{2,1,0:T(8,128)(2,1)S(1)} copy-done((bf16[1,512,128]{2,1,0:T(8,128)(2,1)S(1)}, bf16[1,512,128]{2,1,0:T(8,128)(2,1)}, u32[]{:S(2)}) %copy-start.2) | copy-done | bytes 131096
  4.7 0.0 copy-start.3
  4.7 0.9 %copy-done.3 = bf16[1,512,128]{2,1,0:T(8,128)(2,1)S(1)} copy-done((bf16[1,512,128]{2,1,0:T(8,128)(2,1)S(1)}, bf16[1,512,128]{2,1,0:T(8,128)(2,1)}, u32[]{:S(2)}) %copy-start.3) | copy-done | bytes 131096
  5.6 0.0 copy-start.4
  5.6 0.7 copy-done.4
  6.3 0.0 copy-start.5
  6.3 0.7 copy-done.5
  6.9 68.3 %shard_map.94 = (f32[512,128]{1,0:T(8,128)S(1)}, bf16[224,16,128]{2,1,0:T(8,128)(2,1)S(1)}, bf16[224,16,128]{2,1,0:T(8,128)(2,1)S(1)}) custom-call(bf16[512,128]{1,0:T(8,128)(2,1)S(1)} %bitcast.11, bf16[512,128]{1,0:T(8,128)(2,1)S(1)} %bitcast.12, bf16[27,128,128]{2,1,0:T(8,128)(2,1)S(1)} %copy-done, bf16[27,128,128]{2,1,0:T(8,128)(2,1)S(1)} %copy-done.1, ...), custom_call_target="tpu_custom_call" | custom-call | tf_op jit(solution)/shard_map/pallas_call | solution.py:490
  75.3 2.1 %convert_multiply_fusion = (f32[216,16,128]{2,1,0:T(8,128)}, f32[216,16,128]{2,1,0:T(8,128)}) fusion(bf16[224,16,128]{2,1,0:T(8,128)(2,1)S(1)} %get-tuple-element.8, bf16[224,16,128]{2,1,0:T(8,128)(2,1)S(1)} %get-tuple-element.7), kind=kLoop, calls=%fused_computation | loop fusion | flops 1769472 | bytes 5308416 | tf_op jit(solution)/shard_map/mul | solution.py:538
  77.4 0.7 copy.14
Async XLA Ops:
  1.5 1.2 %copy-start = (bf16[27,128,128]{2,1,0:T(8,128)(2,1)S(1)}, bf16[27,128,128]{2,1,0:T(8,128)(2,1)}, u32[]{:S(2)}) copy-start(bf16[27,128,128]{2,1,0:T(8,128)(2,1)} %weight_one.1) | copy-start | bytes 2654212
  2.6 1.2 %copy-start.1 = (bf16[27,128,128]{2,1,0:T(8,128)(2,1)S(1)}, bf16[27,128,128]{2,1,0:T(8,128)(2,1)}, u32[]{:S(2)}) copy-start(bf16[27,128,128]{2,1,0:T(8,128)(2,1)} %weight_two.1) | copy-start | bytes 2654212
  3.8 0.9 %copy-start.2 = (bf16[1,512,128]{2,1,0:T(8,128)(2,1)S(1)}, bf16[1,512,128]{2,1,0:T(8,128)(2,1)}, u32[]{:S(2)}) copy-start(bf16[1,512,128]{2,1,0:T(8,128)(2,1)} %param.7) | copy-start | bytes 393220
  4.7 0.9 %copy-start.3 = (bf16[1,512,128]{2,1,0:T(8,128)(2,1)S(1)}, bf16[1,512,128]{2,1,0:T(8,128)(2,1)}, u32[]{:S(2)}) copy-start(bf16[1,512,128]{2,1,0:T(8,128)(2,1)} %param.8) | copy-start | bytes 393220
  5.6 0.7 copy-start.4
  6.3 0.7 copy-start.5

commit v4 on v3

--- a/solution.py
+++ b/solution.py
@@ -11,7 +11,7 @@
 BF16 = jnp.bfloat16
 CHUNK = 256
 GROUP = 3
-VMEM_LIMIT = 48 * 1024 * 1024
+VMEM_LIMIT = 62 * 1024 * 1024
 
 
 def dot(a, b):
@@ -95,144 +95,116 @@
     return jnp.concatenate(out, axis=1)
 
 
-class Exchange:
-    def __init__(self, topo, local, land, half_own, half_send, land_quad, quad_send, land_line, out, send_sems, recv_sems):
-        self.topo, self.local, self.land = topo, local, land
-        self.half_own, self.half_send, self.land_quad = half_own, half_send, land_quad
-        self.quad_send, self.land_line, self.out = quad_send, land_line, out
-        self.send_sems, self.recv_sems = send_sems, recv_sems
-        self.half = half_own.shape[0]
-        self.quad = self.half // topo.n_quad
-        self.piece = self.quad // topo.n_line
-        self.next_sem = 0
-
-    def copy(self, src, dst, device):
-        sem = self.next_sem
-        self.next_sem += 1
-        return pltpu.make_async_remote_copy(
-            src_ref=src,
-            dst_ref=dst,
-            send_sem=self.send_sems.at[sem],
-            recv_sem=self.recv_sems.at[sem],
-            device_id=device,
-            device_id_type=pl.DeviceIdType.MESH,
-        )
-
-    def start(self, copies):
-        for copy in copies:
-            copy.start()
-        self.flying = copies
-
-    def land_all(self):
-        for copy in self.flying:
-            copy.wait()
-
-    def stage_core(self):
-        t = self.topo
-        self.start([
-            self.copy(self.local.at[pl.ds((1 - t.core) * self.half, self.half)], self.land, t.device(core=1 - t.core))
-        ])
-
-    def stage_quad(self):
-        t = self.topo
-        self.land_all()
-        total = self.local[pl.ds(t.core * self.half, self.half)] + self.land[...]
-        self.half_own[...] = total
-        self.half_send[...] = total.astype(BF16)
-        copies = []
-        for d in range(1, t.n_quad):
-            q = lax.rem(t.quad + d, t.n_quad)
-            copies.append(self.copy(
-                self.half_send.at[pl.ds(q * self.quad, self.quad)], self.land_quad.at[d - 1], t.device(quad=q)
-            ))
-        self.start(copies)
-
-    def stage_line(self):
-        t = self.topo
-        self.land_all()
-        total = self.half_own[pl.ds(t.quad * self.quad, self.quad)]
-        for d in range(1, t.n_quad):
-            total = total + self.land_quad[d - 1].astype(F32)
-        self.half_own[pl.ds(t.quad * self.quad, self.quad)] = total
-        self.quad_send[...] = total.astype(BF16)
-        copies = []
-        for d in range(1, t.n_line):
-            w = lax.rem(t.line + d, t.n_line)
-            copies.append(self.copy(
-                self.quad_send.at[pl.ds(w * self.piece, self.piece)], self.land_line.at[d - 1], t.device(line=w)
-            ))
-        self.start(copies)
-
-    def stage_share_line(self):
-        t = self.topo
-        self.land_all()
-        total = self.half_own[pl.ds(t.quad * self.quad + t.line * self.piece, self.piece)]
-        for d in range(1, t.n_line):
-            total = total + self.land_line[d - 1].astype(F32)
-        place = pl.ds(t.core * self.half + t.quad * self.quad + t.line * self.piece, self.piece)
-        self.out[place] = total.astype(BF16)
-        self.start([
-            self.copy(self.out.at[place], self.out.at[place], t.device(line=lax.rem(t.line + d, t.n_line)))
-            for d in range(1, t.n_line)
-        ])
-
-    def stage_share_quad(self):
-        t = self.topo
-        self.land_all()
-        place = pl.ds(t.core * self.half + t.quad * self.quad, self.quad)
-        self.start([
-            self.copy(self.out.at[place], self.out.at[place], t.device(quad=lax.rem(t.quad + d, t.n_quad)))
-            for d in range(1, t.n_quad)
-        ])
-
-    def stage_share_core(self):
-        t = self.topo
-        self.land_all()
-        place = pl.ds(t.core * self.half, self.half)
-        self.start([self.copy(self.out.at[place], self.out.at[place], t.device(core=1 - t.core))])
-
-
 class Topology:
     def __init__(self, n_space, n_dp):
         self.n_space, self.n_dp = n_space, n_dp
-        self.n_line = n_space // 2
-        self.n_quad = (n_dp // 2) * 2
+        self.size = {"core": 2, "side": 2, "rank": n_dp // 2, "line": n_space // 2}
         self.space, self.dp = lax.axis_index("space"), lax.axis_index("dp")
-        self.core = lax.rem(self.dp, 2)
-        self.quad = (self.dp // 2) * 2 + lax.rem(self.space, 2)
-        self.line = self.space // 2
-
-    def device(self, core=None, quad=None, line=None):
-        core = self.core if core is None else core
-        quad = self.quad if quad is None else quad
-        line = self.line if line is None else line
-        return (line * 2 + lax.rem(quad, 2), (quad // 2) * 2 + core)
+        self.at = {
+            "core": lax.rem(self.dp, 2), "side": lax.rem(self.space, 2),
+            "rank": self.dp // 2, "line": self.space // 2,
+        }
+
+    def others(self, axis):
+        found = []
+        for d in range(1, self.size[axis]):
+            index = lax.rem(self.at[axis] + d, self.size[axis])
+            at = dict(self.at, **{axis: index})
+            found.append((d - 1, index, (at["line"] * 2 + at["side"], at["rank"] * 2 + at["core"])))
+        return found
 
     def partners(self):
-        found = [self.device(core=1 - self.core)]
-        found += [self.device(quad=lax.rem(self.quad + d, self.n_quad)) for d in range(1, self.n_quad)]
-        found += [self.device(line=lax.rem(self.line + d, self.n_line)) for d in range(1, self.n_line)]
+        found = [device for axis in self.size for _, _, device in self.others(axis)]
         found += [(lax.rem(self.space + d, self.n_space), self.dp) for d in (1, self.n_space - 1)]
         return found
 
 
-def exchange_copies(n_quad, n_line):
-    return 2 * (1 + (n_quad - 1) + (n_line - 1))
+class Exchange:
+    def __init__(self, topo, axes, base, local, out, lands, sends, send_sems, recv_sems):
+        self.topo, self.axes, self.local, self.out = topo, axes, local, out
+        self.lands, self.sends, self.send_sems, self.recv_sems = lands, sends, send_sems, recv_sems
+        self.offset, self.count = base, lands[0].shape[1] * topo.size[axes[0]]
+        self.level, self.sem, self.flying, self.stack = 0, 0, [], []
+
+    def copy(self, src, dst, device):
+        sem, self.sem = self.sem, self.sem + 1
+        made = pltpu.make_async_remote_copy(
+            src_ref=src, dst_ref=dst, send_sem=self.send_sems.at[sem], recv_sem=self.recv_sems.at[sem],
+            device_id=device, device_id_type=pl.DeviceIdType.MESH,
+        )
+        made.start()
+        self.flying.append(made)
+
+    def advance(self):
+        for made in self.flying:
+            made.wait()
+        self.flying = []
+        t, depth = self.topo, len(self.axes)
+        if 0 < self.level <= depth:
+            axis = self.axes[self.level - 1]
+            self.stack.append((self.offset, self.count))
+            self.count //= t.size[axis]
+            self.offset = self.offset + t.at[axis] * self.count
+            own = pl.ds(self.offset, self.count)
+            total = self.local[own]
+            for slot in range(t.size[axis] - 1):
+                total = total + self.lands[self.level - 1][slot].astype(F32)
+            if self.level < depth:
+                self.local[own] = total
+                self.sends[self.level - 1][...] = total.astype(BF16)
+            else:
+                self.out[own] = total.astype(BF16)
+        if self.level < depth:
+            axis = self.axes[self.level]
+            piece = self.count // t.size[axis]
+            for slot, index, device in t.others(axis):
+                if self.level == 0:
+                    src = self.local.at[pl.ds(self.offset + index * piece, piece)]
+                else:
+                    src = self.sends[self.level - 1].at[pl.ds(index * piece, piece)]
+                self.copy(src, self.lands[self.level].at[slot], device)
+        elif self.level < 2 * depth:
+            axis = self.axes[2 * depth - 1 - self.level]
+            place = self.out.at[pl.ds(self.offset, self.count)]
+            for _, _, device in t.others(axis):
+                self.copy(place, place, device)
+            self.offset, self.count = self.stack.pop()
+        self.level += 1
+
+
+def plan_parts(n_space, n_dp, kernels, per):
+    devices = n_space * n_dp
+    units = -(-kernels * per // devices)
+    first = (units + 1) // 2
+    parts = [(0, first * devices, ("core", "side", "rank", "line"))]
+    if units > first:
+        parts.append((first * devices, (units - first) * devices, ("core", "rank", "side", "line")))
+    return parts, units * devices
+
+
+def part_shapes(sizes, tiles, axes, width):
+    lands, sends = [], []
+    for level, axis in enumerate(axes):
+        if level:
+            sends.append(pltpu.VMEM((tiles, 16, width), BF16))
+        tiles //= sizes[axis]
+        lands.append(pltpu.VMEM((sizes[axis] - 1, tiles, 16, width), BF16 if level else F32))
+    return lands, sends
 
 
 def whole_kernel(
     dims, n_space, n_dp,
-    feats, cot, weight_one, weight_two, rules, sends, counts,
+    feats_hbm, cot_hbm, one_hbm, two_hbm, rules_hbm, sends_hbm, counts_hbm,
     grad_rows, out_one, out_two,
+    feats, cot, weight_one, weight_two, rules, sends, counts, load_sems,
     xa_t, ga_t, gga, gx, prod, ext, z, slope, dz, dext, dext_rim, rim_low, rim_high, rim32, halo_bf, halo_f32, low_rows, chunk_rows,
-    local_one, local_two, land, half_own, half_send, land_quad, quad_send, land_line,
-    send_sems, recv_sems, halo_send_sems, halo_recv_sems,
+    local_one, local_two, send_sems, recv_sems, halo_send_sems, halo_recv_sems, *part_refs,
 ):
     blocks, block, per_side = dims
     rows, width = feats.shape
     halo = per_side * block
     ext_rows = rows + 2 * halo
-    kernels, slots = rules.shape[1:]
+    kernels, _, slots = rules.shape
     groups = kernels // GROUP
     own_chunks, ext_chunks = rows // CHUNK, ext_rows // CHUNK
 
@@ -256,12 +228,23 @@
     topo = Topology(n_space, n_dp)
     barrier = pltpu.get_barrier_semaphore()
     partners = topo.partners()
+    loads = [
+        pltpu.make_async_copy(src, dst, load_sems.at[i])
+        for i, (src, dst) in enumerate((
+            (sends_hbm, sends), (counts_hbm, counts), (rules_hbm, rules), (feats_hbm, feats),
+            (cot_hbm, cot), (two_hbm, weight_two), (one_hbm, weight_one),
+        ))
+    ]
+    for load in loads:
+        load.start()
     for device in partners:
         pl.semaphore_signal(barrier, inc=1, device_id=device, device_id_type=pl.DeviceIdType.MESH)
 
+    for load in loads[:5]:
+        load.wait()
     mask = jnp.concatenate(active_mask(counts, blocks, block, width), axis=1)
     for kind, limit in ((0, ext_rows), (1, rows)):
-        index = rules[kind]
+        index = rules[:, kind, :]
         low_rows[kind] = jnp.where(index < limit, lax.rem(index, CHUNK), -1).astype(F32)
         chunk_rows[kind] = (index // CHUNK).astype(F32)
     xa = feats[...].astype(F32).T * mask
@@ -281,10 +264,10 @@
             halo_f32[s, 1] = jnp.zeros((width, halo), F32)
 
     per = width // 16
-    pad = (local_one.shape[0] // per) - kernels
+    pad = local_one.shape[0] - kernels * per
     for local in (local_one, local_two):
         if pad:
-            local[pl.ds(kernels * per, pad * per)] = jnp.zeros((pad * per, 16, width), F32)
+            local[pl.ds(kernels * per, pad)] = jnp.zeros((pad, 16, width), F32)
     pl.semaphore_wait(barrier, len(partners))
 
     def halo_copies(which, to_low, to_high, landing):
@@ -328,6 +311,7 @@
     x_copies = halo_copies(0, rim_low.at[0], rim_high.at[0], halo_bf.at[0])
     halo_start(x_copies)
 
+    loads[5].wait()
     dext[...] = jnp.zeros_like(dext)
 
     def back_two(i, _):
@@ -352,6 +336,7 @@
     dy_copies = halo_copies(1, dext_rim.at[0, 0], dext_rim.at[0, 1], halo_f32.at[0])
     halo_start(dy_copies)
 
+    loads[6].wait()
     halo_wait(x_copies)
     ext[pl.ds(0, own_chunks * width)] = xa_t[...]
     set_rim(ext, 0, halo_bf[0, 0])
@@ -400,17 +385,34 @@
             prod[k] = dot(weight_one[k], gathered).astype(BF16)
         return 0
 
-    lax.fori_loop(0, groups, grad_first, 0)
-
-    def exchange(side, local, out):
-        return Exchange(
-            topo, local, land.at[side], half_own.at[side], half_send.at[side], land_quad.at[side],
-            quad_send.at[side], land_line.at[side], out, send_sems.at[side], recv_sems.at[side],
-        )
-
-    one = exchange(0, local_one, out_one)
-    two = exchange(1, local_two, out_two)
-    one.stage_core()
+    plan, _ = plan_parts(n_space, n_dp, kernels, per)
+    depth = len(plan[0][2])
+    parts = [None] * 4
+    refs = iter(part_refs)
+    sem_row = 0
+    for side, (local, out) in enumerate(((local_one, out_one), (local_two, out_two))):
+        for i, (base, _, axes) in enumerate(plan):
+            lands = [next(refs) for _ in range(depth)]
+            stages = [next(refs) for _ in range(depth - 1)]
+            parts[2 * side + i] = Exchange(
+                topo, axes, base, local, out, lands, stages, send_sems.at[sem_row], recv_sems.at[sem_row]
+            )
+            sem_row += 1
+    cut = min(groups, -(-plan[0][1] // (per * GROUP)))
+
+    def go(*which):
+        for p in which:
+            if parts[p] is not None:
+                parts[p].advance()
+
+    def run(start, stop, step):
+        if start < stop:
+            lax.fori_loop(start, stop, step, 0)
+
+    run(0, cut, grad_first)
+    go(0)
+    run(cut, groups, grad_first)
+    go(1, 0)
 
     halo_wait(y_copies)
     set_rim(ext, 0, halo_bf[1, 0])
@@ -423,12 +425,10 @@
             local_two[pl.ds(k * per, per)] = dot_nt(gathered, gga[k]).reshape(per, 16, width)
         return 0
 
-    cut = (2 * groups) // 3
-    lax.fori_loop(0, cut, grad_second, 0)
-    one.stage_quad()
-    lax.fori_loop(cut, groups, grad_second, 0)
-    two.stage_core()
-
+    run(0, cut, grad_second)
+    go(2, 1)
+    run(cut, groups, grad_second)
+    go(3, 0, 2)
     dext[...] = jnp.zeros_like(dext)
 
     def back_one(i, _):
@@ -441,29 +441,23 @@
         return 0
 
     cut_a, cut_b = groups // 3, (2 * groups) // 3
-    lax.fori_loop(0, cut_a, back_one, 0)
-    two.stage_quad()
-    one.stage_line()
-    lax.fori_loop(cut_a, cut_b, back_one, 0)
-    one.stage_share_line()
-    lax.fori_loop(cut_b, groups, back_one, 0)
+    run(0, cut_a, back_one)
+    go(1, 3)
+    run(cut_a, cut_b, back_one)
+    go(0, 2)
+    run(cut_b, groups, back_one)
     dext_rim[1, 0] = rim_part(dext, 0)
     dext_rim[1, 1] = rim_part(dext, 1)
     dx_copies = halo_copies(3, dext_rim.at[1, 0], dext_rim.at[1, 1], halo_f32.at[1])
     halo_start(dx_copies)
-    two.stage_line()
-    one.stage_share_quad()
+    go(1, 3, 0, 2, 1, 0)
     halo_wait(dx_copies)
     own = add_back(
         own_part(dext), sends, per_side, halo_f32[1, 0], halo_f32[1, 1], blocks, block
     )
     grad_rows[...] = (own * mask).T
-    two.stage_share_line()
-    one.stage_share_core()
-    two.stage_share_quad()
-    one.land_all()
-    two.stage_share_core()
-    two.land_all()
+    go(3, 2, 1, 0, 3, 2, 1, 0, 3, 2, 1, 3, 2, 0, 3, 1, 2, 3)
+    assert all(p is None or p.level == 2 * depth + 1 for p in parts)
 
 
 def body(n_space, n_dp, features, cotangent, weight_one, weight_two, rules, halo_send, block_counts):
@@ -477,15 +471,14 @@
     ext_rows = rows + 2 * halo
     per = width // 16
     devices = n_space * n_dp
-    padded = kernels
-    while (padded * per) % devices:
-        padded += 1
-    tiles = padded * per
-    half = tiles // 2
-    n_quad, n_line = (n_dp // 2) * 2, n_space // 2
-    quad = half // n_quad
-    piece = quad // n_line
-    copies = exchange_copies(n_quad, n_line)
+    plan, tiles = plan_parts(n_space, n_dp, kernels, per)
+    sizes = {"core": 2, "side": 2, "rank": n_dp // 2, "line": n_space // 2}
+    copies = 2 * sum(n - 1 for n in sizes.values())
+    part_scratch = []
+    for _ in range(2):
+        for _, count, axes in plan:
+            lands, stages = part_shapes(sizes, count, axes, width)
+            part_scratch += lands + stages
     v, s = pltpu.VMEM, pltpu.SMEM
     grad_rows, one, two = pl.pallas_call(
         functools.partial(whole_kernel, (blocks, block, per_side), n_space, n_dp),
@@ -494,9 +487,17 @@
             jax.ShapeDtypeStruct((tiles, 16, width), BF16),
             jax.ShapeDtypeStruct((tiles, 16, width), BF16),
         ],
-        in_specs=[pl.BlockSpec(memory_space=m) for m in (v, v, v, v, v, s, s)],
+        in_specs=[pl.BlockSpec(memory_space=pl.ANY)] * 7,
         out_specs=[pl.BlockSpec(memory_space=v)] * 3,
         scratch_shapes=[
+            v((rows, width), BF16),
+            v((rows, width), BF16),
+            v((kernels, width, width), BF16),
+            v((kernels, width, width), BF16),
+            v((kernels, 2, slots), jnp.int32),
+            s((2, per_side), jnp.int32),
+            s((1, blocks), jnp.int32),
+            pltpu.SemaphoreType.DMA((7,)),
             v((width * rows // CHUNK, CHUNK), BF16),
             v((width * rows // CHUNK, CHUNK), BF16),
             v((kernels, width, slots), BF16),
@@ -517,21 +518,16 @@
             v((2, kernels, slots), F32),
             v((tiles, 16, width), F32),
             v((tiles, 16, width), F32),
-            v((2, half, 16, width), F32),
-            v((2, half, 16, width), F32),
-            v((2, half, 16, width), BF16),
-            v((2, n_quad - 1, quad, 16, width), BF16),
-            v((2, quad, 16, width), BF16),
-            v((2, n_line - 1, piece, 16, width), BF16),
-            pltpu.SemaphoreType.DMA((2, copies)),
-            pltpu.SemaphoreType.DMA((2, copies)),
+            pltpu.SemaphoreType.DMA((2 * len(plan), copies)),
+            pltpu.SemaphoreType.DMA((2 * len(plan), copies)),
             pltpu.SemaphoreType.DMA((4, 2)),
             pltpu.SemaphoreType.DMA((4, 2)),
+            *part_scratch,
         ],
         compiler_params=pltpu.CompilerParams(
             collective_id=0, has_side_effects=True, vmem_limit_bytes=VMEM_LIMIT
         ),
-    )(feats, cot, weight_one, weight_two, links, sends, block_counts)
+    )(feats, cot, weight_one, weight_two, links.transpose(1, 0, 2), sends, block_counts)
     scale = 1.0 / jnp.sqrt(F32(devices * slots))
 
     def finish(total):

time: 78.4 us -> 76.4 us (0.974)
  local copies, waits for them, and re-layouts: 7 us -> 0.71 us
  Pallas kernels: 68.3 us -> 71.3 us
  other arithmetic: 2.1 us -> 3.58 us
    unnamed x14 -> x3, local copies, waits for them, and re-layouts: 7 us -> 0.71 us
    pallas_call x1, Pallas kernels: 68.3 us -> 71.3 us  [body(): pl.pallas_call(functools.partial(whole_kernel, (blocks, block, per_side),...]
    mul x1, other arithmetic: 2.1 us -> 3.58 us  [finish(): total[:kernels * per].astype(F32).reshape(kernels, width, width) * scale]
where the time goes in v4:
time: 76.4 us; the launch traced here: 76.2 us
  Pallas kernels  71.3 us (93%)
  other arithmetic  3.58 us (5%)
    pallas_call x1, Pallas kernels, body(): pl.pallas_call(functools.partial(whole_kernel, (blocks, block, per_side),...  71.3 us
    mul x1, other arithmetic, finish(): total[:kernels * per].astype(F32).reshape(kernels, width, width) * scale  3.58 us

profile of v4, /device:TPU:0, one launch (start us, length us, event | category | flops | bytes accessed | tf_op | source)
XLA Modules:
  0.0 76.2 jit_solution(14183727288768316622)
XLA Ops:
  0.6 71.3 %shard_map.94 = (f32[512,128]{1,0:T(8,128)}, bf16[224,16,128]{2,1,0:T(8,128)(2,1)}, bf16[224,16,128]{2,1,0:T(8,128)(2,1)}) custom-call(bf16[512,128]{1,0:T(8,128)(2,1)} %bitcast.12, bf16[512,128]{1,0:T(8,128)(2,1)} %bitcast.13, bf16[27,128,128]{2,1,0:T(8,128)(2,1)} %one_hbm.1, bf16[27,128,128]{2,1,0:T(8,128)(2,1)} %two_hbm.1, s32[27,2,256]{2,1,0:T(2,128)} %bitcast.14, ...), custom_call_target="tpu_custom_call" | custom-call | tf_op jit(solution)/shard_map/pallas_call | solution.py:483
  71.9 0.0 copy-start
  71.9 3.6 %convert_multiply_fusion = (f32[216,16,128]{2,1,0:T(8,128)}, f32[216,16,128]{2,1,0:T(8,128)}) fusion(bf16[224,16,128]{2,1,0:T(8,128)(2,1)} %get-tuple-element.8, bf16[224,16,128]{2,1,0:T(8,128)(2,1)} %get-tuple-element.7), kind=kLoop, calls=%fused_computation | loop fusion | flops 1769472 | bytes 5308416 | tf_op jit(solution)/shard_map/mul | solution.py:534
  75.5 0.0 copy-done
  75.5 0.7 copy.11
Async XLA Ops:
  71.9 3.6 %copy-start = (f32[512,128]{1,0:T(8,128)S(1)}, f32[512,128]{1,0:T(8,128)}, u32[]{:S(2)}) copy-start(f32[512,128]{1,0:T(8,128)} %get-tuple-element.6) | copy-start | bytes 786436

commit v5 on v4

--- a/solution.py
+++ b/solution.py
@@ -10,7 +10,7 @@
 F32 = jnp.float32
 BF16 = jnp.bfloat16
 CHUNK = 256
-GROUP = 3
+GROUP = 9
 VMEM_LIMIT = 62 * 1024 * 1024
 
 
@@ -314,20 +314,22 @@
     loads[5].wait()
     dext[...] = jnp.zeros_like(dext)
 
+    def members(i):
+        return [i * GROUP + j for j in range(GROUP)]
+
     def back_two(i, _):
-        weights, placed = [], []
-        for j in range(GROUP):
-            k = i * GROUP + j
-            found = gather(ga_t[...], selector(1, k), chunk_of(1, k), width)
-            gga[k] = found
-            placed.append(
-                dot_nt(spread(found, chunk_of(0, k), ext_chunks), selector(0, k)).astype(BF16)
-            )
-            weights.append(weight_two[k])
-        weights = jnp.concatenate(weights, axis=1)
+        ks = members(i)
+        found = [gather(ga_t[...], selector(1, k), chunk_of(1, k), width) for k in ks]
+        placed = [
+            dot_nt(spread(f, chunk_of(0, k), ext_chunks), selector(0, k)).astype(BF16)
+            for f, k in zip(found, ks)
+        ]
+        weights = jnp.concatenate([weight_two[k] for k in ks], axis=1)
         for c in range(ext_chunks):
             part = slice(c * width, (c + 1) * width)
             dext[part] += dot(weights, jnp.concatenate([p[part] for p in placed], axis=0))
+        for f, k in zip(found, ks):
+            gga[k] = f
         return 0
 
     lax.fori_loop(0, groups, back_two, 0)
@@ -344,19 +346,18 @@
     z[...] = jnp.zeros_like(z)
 
     def forward(i, _):
-        weights, placed = [], []
-        for j in range(GROUP):
-            k = i * GROUP + j
-            found = gather(ext[...], selector(0, k), chunk_of(0, k), width)
-            gx[k] = found
-            placed.append(
-                dot_nt(spread(found, chunk_of(1, k), own_chunks), selector(1, k)).astype(BF16)
-            )
-            weights.append(weight_one[k])
-        weights = jnp.concatenate(weights, axis=0)
+        ks = members(i)
+        found = [gather(ext[...], selector(0, k), chunk_of(0, k), width) for k in ks]
+        placed = [
+            dot_nt(spread(f, chunk_of(1, k), own_chunks), selector(1, k)).astype(BF16)
+            for f, k in zip(found, ks)
+        ]
+        weights = jnp.concatenate([weight_one[k] for k in ks], axis=0)
         for c in range(own_chunks):
             part = slice(c * width, (c + 1) * width)
             z[part] += dot_tn(weights, jnp.concatenate([p[part] for p in placed], axis=0))
+        for f, k in zip(found, ks):
+            gx[k] = f
         return 0
 
     lax.fori_loop(0, groups, forward, 0)
@@ -378,11 +379,13 @@
     dz[...] = stack((dy * slope[...]).astype(BF16))
 
     def grad_first(i, _):
-        for j in range(GROUP):
-            k = i * GROUP + j
-            gathered = gather(dz[...], selector(1, k), chunk_of(1, k), width)
-            local_one[pl.ds(k * per, per)] = dot_nt(gx[k], gathered).reshape(per, 16, width)
-            prod[k] = dot(weight_one[k], gathered).astype(BF16)
+        ks = members(i)
+        found = [gather(dz[...], selector(1, k), chunk_of(1, k), width) for k in ks]
+        grads = [dot_nt(gx[k], f) for f, k in zip(found, ks)]
+        products = [dot(weight_one[k], f).astype(BF16) for f, k in zip(found, ks)]
+        for grad, product, k in zip(grads, products, ks):
+            local_one[pl.ds(k * per, per)] = grad.reshape(per, 16, width)
+            prod[k] = product
         return 0
 
     plan, _ = plan_parts(n_space, n_dp, kernels, per)
@@ -419,10 +422,11 @@
     set_rim(ext, 1, halo_bf[1, 1])
 
     def grad_second(i, _):
-        for j in range(GROUP):
-            k = i * GROUP + j
-            gathered = gather(ext[...], selector(0, k), chunk_of(0, k), width)
-            local_two[pl.ds(k * per, per)] = dot_nt(gathered, gga[k]).reshape(per, 16, width)
+        ks = members(i)
+        found = [gather(ext[...], selector(0, k), chunk_of(0, k), width) for k in ks]
+        grads = [dot_nt(f, gga[k]) for f, k in zip(found, ks)]
+        for grad, k in zip(grads, ks):
+            local_two[pl.ds(k * per, per)] = grad.reshape(per, 16, width)
         return 0
 
     run(0, cut, grad_second)
@@ -432,12 +436,10 @@
     dext[...] = jnp.zeros_like(dext)
 
     def back_one(i, _):
-        products, selectors = [], []
-        for j in range(GROUP):
-            k = i * GROUP + j
-            products.append(spread(prod[k], chunk_of(0, k), ext_chunks))
-            selectors.append(selector(0, k))
-        dext[...] += dot_nt(jnp.concatenate(products, axis=1), jnp.concatenate(selectors, axis=1))
+        ks = members(i)
+        spreads = [spread(prod[k], chunk_of(0, k), ext_chunks) for k in ks]
+        selectors = [selector(0, k) for k in ks]
+        dext[...] += dot_nt(jnp.concatenate(spreads, axis=1), jnp.concatenate(selectors, axis=1))
         return 0
 
     cut_a, cut_b = groups // 3, (2 * groups) // 3

time: 76.4 us -> 65.5 us (0.86)
  Pallas kernels: 71.3 us -> 60.4 us
    pallas_call x1, Pallas kernels: 71.3 us -> 60.4 us  [body(): pl.pallas_call(functools.partial(whole_kernel, (blocks, block, per_side),...]
where the time goes in v5:
time: 65.5 us; the launch traced here: 65.4 us
  Pallas kernels  60.4 us (92%)
  other arithmetic  3.58 us (5%)
  local copies, waits for them, and re-layouts  0.71 us (1%)
    pallas_call x1, Pallas kernels, body(): pl.pallas_call(functools.partial(whole_kernel, (blocks, block, per_side),...  60.4 us
    mul x1, other arithmetic, finish(): total[:kernels * per].astype(F32).reshape(kernels, width, width) * scale  3.58 us

profile of v5, /device:TPU:0, one launch (start us, length us, event | category | flops | bytes accessed | tf_op | source)
XLA Modules:
  0.0 65.4 jit_solution(9385695200497026886)
XLA Ops:
  0.6 60.4 %shard_map.94 = (f32[512,128]{1,0:T(8,128)}, bf16[224,16,128]{2,1,0:T(8,128)(2,1)}, bf16[224,16,128]{2,1,0:T(8,128)(2,1)}) custom-call(bf16[512,128]{1,0:T(8,128)(2,1)} %bitcast.12, bf16[512,128]{1,0:T(8,128)(2,1)} %bitcast.13, bf16[27,128,128]{2,1,0:T(8,128)(2,1)} %one_hbm.1, bf16[27,128,128]{2,1,0:T(8,128)(2,1)} %two_hbm.1, s32[27,2,256]{2,1,0:T(2,128)} %bitcast.14, ...), custom_call_target="tpu_custom_call" | custom-call | tf_op jit(solution)/shard_map/pallas_call | solution.py:485
  61.1 0.0 copy-start
  61.1 3.6 %convert_multiply_fusion = (f32[216,16,128]{2,1,0:T(8,128)}, f32[216,16,128]{2,1,0:T(8,128)}) fusion(bf16[224,16,128]{2,1,0:T(8,128)(2,1)} %get-tuple-element.8, bf16[224,16,128]{2,1,0:T(8,128)(2,1)} %get-tuple-element.7), kind=kLoop, calls=%fused_computation | loop fusion | flops 1769472 | bytes 5308416 | tf_op jit(solution)/shard_map/mul | solution.py:536
  64.7 0.0 copy-done
  64.7 0.7 %copy.11 = f32[1,512,128]{2,1,0:T(8,128)} copy(f32[1,512,128]{2,1,0:T(8,128)S(1)} %bitcast.11) | data formatting | bytes 524288
Async XLA Ops:
  61.1 3.6 %copy-start = (f32[512,128]{1,0:T(8,128)S(1)}, f32[512,128]{1,0:T(8,128)}, u32[]{:S(2)}) copy-start(f32[512,128]{1,0:T(8,128)} %get-tuple-element.6) | copy-start | bytes 786436

commit v6 on v5

--- a/solution.py
+++ b/solution.py
@@ -98,11 +98,12 @@
 class Topology:
     def __init__(self, n_space, n_dp):
         self.n_space, self.n_dp = n_space, n_dp
-        self.size = {"core": 2, "side": 2, "rank": n_dp // 2, "line": n_space // 2}
+        self.size = {"core": 2, "quad": (n_dp // 2) * 2, "line": n_space // 2}
         self.space, self.dp = lax.axis_index("space"), lax.axis_index("dp")
         self.at = {
-            "core": lax.rem(self.dp, 2), "side": lax.rem(self.space, 2),
-            "rank": self.dp // 2, "line": self.space // 2,
+            "core": lax.rem(self.dp, 2),
+            "quad": (self.dp // 2) * 2 + lax.rem(self.space, 2),
+            "line": self.space // 2,
         }
 
     def others(self, axis):
@@ -110,7 +111,8 @@
         for d in range(1, self.size[axis]):
             index = lax.rem(self.at[axis] + d, self.size[axis])
             at = dict(self.at, **{axis: index})
-            found.append((d - 1, index, (at["line"] * 2 + at["side"], at["rank"] * 2 + at["core"])))
+            device = (at["line"] * 2 + lax.rem(at["quad"], 2), (at["quad"] // 2) * 2 + at["core"])
+            found.append((d - 1, index, device))
         return found
 
     def partners(self):
@@ -151,17 +153,17 @@
                 total = total + self.lands[self.level - 1][slot].astype(F32)
             if self.level < depth:
                 self.local[own] = total
-                self.sends[self.level - 1][...] = total.astype(BF16)
+                self.sends[self.level][...] = total.astype(BF16)
             else:
                 self.out[own] = total.astype(BF16)
         if self.level < depth:
             axis = self.axes[self.level]
             piece = self.count // t.size[axis]
             for slot, index, device in t.others(axis):
+                part = pl.ds(index * piece, piece)
+                src = self.sends[self.level].at[part]
                 if self.level == 0:
-                    src = self.local.at[pl.ds(self.offset + index * piece, piece)]
-                else:
-                    src = self.sends[self.level - 1].at[pl.ds(index * piece, piece)]
+                    src[...] = self.local[pl.ds(self.offset + index * piece, piece)].astype(BF16)
                 self.copy(src, self.lands[self.level].at[slot], device)
         elif self.level < 2 * depth:
             axis = self.axes[2 * depth - 1 - self.level]
@@ -176,19 +178,18 @@
     devices = n_space * n_dp
     units = -(-kernels * per // devices)
     first = (units + 1) // 2
-    parts = [(0, first * devices, ("core", "side", "rank", "line"))]
+    parts = [(0, first * devices, ("core", "quad", "line"))]
     if units > first:
-        parts.append((first * devices, (units - first) * devices, ("core", "rank", "side", "line")))
+        parts.append((first * devices, (units - first) * devices, ("core", "quad", "line")))
     return parts, units * devices
 
 
 def part_shapes(sizes, tiles, axes, width):
     lands, sends = [], []
     for level, axis in enumerate(axes):
-        if level:
-            sends.append(pltpu.VMEM((tiles, 16, width), BF16))
+        sends.append(pltpu.VMEM((tiles, 16, width), BF16))
         tiles //= sizes[axis]
-        lands.append(pltpu.VMEM((sizes[axis] - 1, tiles, 16, width), BF16 if level else F32))
+        lands.append(pltpu.VMEM((sizes[axis] - 1, tiles, 16, width), BF16))
     return lands, sends
 
 
@@ -396,7 +397,7 @@
     for side, (local, out) in enumerate(((local_one, out_one), (local_two, out_two))):
         for i, (base, _, axes) in enumerate(plan):
             lands = [next(refs) for _ in range(depth)]
-            stages = [next(refs) for _ in range(depth - 1)]
+            stages = [next(refs) for _ in range(depth)]
             parts[2 * side + i] = Exchange(
                 topo, axes, base, local, out, lands, stages, send_sems.at[sem_row], recv_sems.at[sem_row]
             )
@@ -458,7 +459,7 @@
         own_part(dext), sends, per_side, halo_f32[1, 0], halo_f32[1, 1], blocks, block
     )
     grad_rows[...] = (own * mask).T
-    go(3, 2, 1, 0, 3, 2, 1, 0, 3, 2, 1, 3, 2, 0, 3, 1, 2, 3)
+    go(3, 2, 1, 0, 3, 2, 1, 3, 2, 3)
     assert all(p is None or p.level == 2 * depth + 1 for p in parts)
 
 
@@ -474,7 +475,7 @@
     per = width // 16
     devices = n_space * n_dp
     plan, tiles = plan_parts(n_space, n_dp, kernels, per)
-    sizes = {"core": 2, "side": 2, "rank": n_dp // 2, "line": n_space // 2}
+    sizes = {"core": 2, "quad": (n_dp // 2) * 2, "line": n_space // 2}
     copies = 2 * sum(n - 1 for n in sizes.values())
     part_scratch = []
     for _ in range(2):

time: 65.5 us -> 60.5 us (0.924)
  Pallas kernels: 60.4 us -> 55.4 us
    pallas_call x1, Pallas kernels: 60.4 us -> 55.4 us  [body(): pl.pallas_call(functools.partial(whole_kernel, (blocks, block, per_side),...]
where the time goes in v6:
time: 60.5 us; the launch traced here: 60.3 us
  Pallas kernels  55.4 us (92%)
  other arithmetic  3.58 us (6%)
  local copies, waits for them, and re-layouts  0.71 us (1%)
  between operations  0.65 us (1%)
    pallas_call x1, Pallas kernels, body(): pl.pallas_call(functools.partial(whole_kernel, (blocks, block, per_side),...  55.4 us
    mul x1, other arithmetic, finish(): total[:kernels * per].astype(F32).reshape(kernels, width, width) * scale  3.58 us

profile of v6, /device:TPU:0, one launch (start us, length us, event | category | flops | bytes accessed | tf_op | source)
XLA Modules:
  0.0 60.3 jit_solution(17097880661168226993)
XLA Ops:
  0.6 55.4 %shard_map.94 = (f32[512,128]{1,0:T(8,128)}, bf16[224,16,128]{2,1,0:T(8,128)(2,1)}, bf16[224,16,128]{2,1,0:T(8,128)(2,1)}) custom-call(bf16[512,128]{1,0:T(8,128)(2,1)} %bitcast.12, bf16[512,128]{1,0:T(8,128)(2,1)} %bitcast.13, bf16[27,128,128]{2,1,0:T(8,128)(2,1)} %one_hbm.1, bf16[27,128,128]{2,1,0:T(8,128)(2,1)} %two_hbm.1, s32[27,2,256]{2,1,0:T(2,128)} %bitcast.14, ...), custom_call_target="tpu_custom_call" | custom-call | tf_op jit(solution)/shard_map/pallas_call | solution.py:486
  56.0 0.0 copy-start
  56.0 3.6 %convert_multiply_fusion = (f32[216,16,128]{2,1,0:T(8,128)}, f32[216,16,128]{2,1,0:T(8,128)}) fusion(bf16[224,16,128]{2,1,0:T(8,128)(2,1)} %get-tuple-element.8, bf16[224,16,128]{2,1,0:T(8,128)(2,1)} %get-tuple-element.7), kind=kLoop, calls=%fused_computation | loop fusion | flops 1769472 | bytes 5308416 | tf_op jit(solution)/shard_map/mul | solution.py:537
  59.6 0.0 copy-done
  59.6 0.7 %copy.11 = f32[1,512,128]{2,1,0:T(8,128)} copy(f32[1,512,128]{2,1,0:T(8,128)S(1)} %bitcast.11) | data formatting | bytes 524288
Async XLA Ops:
  56.0 3.6 %copy-start = (f32[512,128]{1,0:T(8,128)S(1)}, f32[512,128]{1,0:T(8,128)}, u32[]{:S(2)}) copy-start(f32[512,128]{1,0:T(8,128)} %get-tuple-element.6) | copy-start | bytes 786436
